TPU v7x, 256 devices: a whole 4x4x8 slice. The times are simulated.
256 devices in a mesh: chan: 128 (over z, x, y_lo, core), tile: 2 (over y_hi).
Axes of the slice: x: 4, y: 4 (y_hi: 2, y_lo: 2; y = y_hi * 2 + y_lo), z: 8, core: 2. Of those that a mesh axis runs over, the one named last changes fastest.
Arguments:
- voltages: bfloat16 [2, 512, 2, 454656], P(None, 'chan', 'tile'), may hold values from -6 to 6
- filter_taps: float32 [16, 4096], replicated, may hold values from -1.5 to 1.5
- input_good: int32 [512, 2], replicated, may hold values 0 or 1
Outputs:
- visibilities: bfloat16 [256, 8, 512, 512], P('chan', None, 'tile')
All inputs are finite; a program needn't handle non-finite values.
Results may differ from a plain program's by a relative error of at most 0.001.
Values sent between devices are 32-bit elements; how exact they have to be, the bound alone decides.
No kernel may reach another device: no remote copies, remote signals or barrier semaphores. Data moves between devices by JAX's collectives and lax.ppermute only.
A program may use at most 128 MiB of HBM per device.

v0:
```python
import math

import jax
import jax.numpy as jnp
from jax import lax
from jax.sharding import PartitionSpec as P

ROOT = 64
CH_DEV = 2


def stokes_planes(corr_real, corr_imag):
    xx_real = corr_real[..., 0, 0, :, :]
    xy_real = corr_real[..., 0, 1, :, :]
    yx_real = corr_real[..., 1, 0, :, :]
    yy_real = corr_real[..., 1, 1, :, :]
    xx_imag = corr_imag[..., 0, 0, :, :]
    xy_imag = corr_imag[..., 0, 1, :, :]
    yx_imag = corr_imag[..., 1, 0, :, :]
    yy_imag = corr_imag[..., 1, 1, :, :]
    planes = (
        xx_real + yy_real,
        xx_real - yy_real,
        xy_real + yx_real,
        xy_imag - yx_imag,
        xx_imag + yy_imag,
        xx_imag - yy_imag,
        xy_imag + yx_imag,
        yx_real - xy_real,
    )
    return jnp.stack(planes, axis=-3).astype(jnp.bfloat16)


def cosine_table(first, second, modulus):
    angle = 2.0 * math.pi / modulus * (first * second % modulus).astype(jnp.float32)
    return (jnp.cos(angle), jnp.sin(angle))


def on_device(voltages, filter_taps, input_good):
    highest = lax.Precision.HIGHEST
    channels = filter_taps.shape[1]
    tap_count = filter_taps.shape[0]
    stations_here = voltages.shape[1] * voltages.shape[2]
    frame_count = voltages.shape[3] // channels
    spectra_count = frame_count - tap_count + 1
    wanted = CH_DEV * lax.axis_size("chan")
    radix_one = ROOT
    radix_two = channels // ROOT
    frames = voltages.reshape(2, stations_here, frame_count, channels)

    def add_tap(tap_index, total):
        window = lax.dynamic_slice_in_dim(frames, tap_index, spectra_count, 2).astype(jnp.float32)
        weight = lax.dynamic_index_in_dim(filter_taps, tap_index, 0, keepdims=False)
        return total + window * weight

    start_sum = jnp.zeros((2, stations_here, spectra_count, channels), jnp.float32)
    filtered = lax.fori_loop(0, tap_count, add_tap, start_sum)
    shaped = filtered.reshape(2, stations_here, spectra_count, radix_one, radix_two)
    real_in = shaped[0]
    imag_in = shaped[1]
    first_rows = jnp.arange(radix_one, dtype=jnp.int32)
    second_rows = jnp.arange(radix_two, dtype=jnp.int32)
    cos_one, sin_one = cosine_table(first_rows[:, None], first_rows[None, :], radix_one)

    def section_one(data, table):
        return jnp.einsum("lsab,ak->lsbk", data, table, precision=highest)

    real_mid = section_one(real_in, cos_one) + section_one(imag_in, sin_one)
    imag_mid = section_one(imag_in, cos_one) - section_one(real_in, sin_one)
    cos_turn, sin_turn = cosine_table(second_rows[:, None], first_rows[None, :], channels)
    real_turned = real_mid * cos_turn + imag_mid * sin_turn
    imag_turned = imag_mid * cos_turn - real_mid * sin_turn
    needed = -(-wanted // radix_one)
    outer_rows = jnp.arange(needed, dtype=jnp.int32)
    cos_two, sin_two = cosine_table(second_rows[:, None], outer_rows[None, :], radix_two)

    def section_two(data, table):
        return jnp.einsum("lsbk,bj->jkls", data, table, precision=highest)

    scale = 1.0 / math.sqrt(channels)
    real_out = (section_two(real_turned, cos_two) + section_two(imag_turned, sin_two)).reshape(
        needed * radix_one, stations_here, spectra_count
    ) * scale
    imag_out = (section_two(imag_turned, cos_two) - section_two(real_turned, sin_two)).reshape(
        needed * radix_one, stations_here, spectra_count
    ) * scale
    moved = jnp.concatenate((real_out, imag_out), axis=2)
    paired = lax.all_gather(moved[:, None], "tile", axis=1, tiled=True)
    joined = lax.all_to_all(paired, "chan", split_axis=0, concat_axis=2, tiled=True)
    mask = input_good.astype(jnp.float32).T
    joined = joined * mask[None, :, :, None]
    half = joined.shape[2] // lax.axis_size("tile")
    rows = lax.dynamic_slice_in_dim(joined, lax.axis_index("tile") * half, half, 2)
    rotated = jnp.concatenate((rows[..., spectra_count:], -rows[..., :spectra_count]), axis=-1)
    corr_real = jnp.einsum("cpax,cqbx->cpqab", rows, joined, precision=highest) / spectra_count
    corr_imag = jnp.einsum("cpax,cqbx->cpqab", rotated, joined, precision=highest) / spectra_count
    return stokes_planes(corr_real, corr_imag)


def solution(mesh):
    in_specs = (P(None, "chan", "tile", None), P(), P())
    out_specs = P("chan", None, "tile", None)
    return jax.shard_map(
        on_device, mesh=mesh, in_specs=in_specs, out_specs=out_specs, check_vma=False
    )
```

profile of v0, /device:TPU:1, one launch (start us, length us, event | category | flops | bytes accessed | tf_op | source)
XLA Modules:
  0.0 509.9 jit_solution(402079473309333113)
XLA Ops:
  6.8 8.4 %reshape.205 = bf16[2,4,111,4096]{3,2,1,0:T(8,128)(2,1)} reshape(bf16[2,4,1,454656]{3,1,2,0:T(4,128)(2,1)} %param.5) | data formatting | bytes 14548992 | tf_op jit(solution)/shard_map/reshape | solution.py:49
  15.2 220.6 %while.14 = (s32[]{:T(128)}, f32[2,4,96,4096]{3,2,1,0:T(8,128)}, bf16[2,4,111,4096]{3,2,1,0:T(8,128)(2,1)}, f32[16,4096]{1,0:T(8,128)}, s32[]{:T(128)}, /*index=5*/s32[]{:T(128)}) while((s32[]{:T(128)}, f32[2,4,96,4096]{3,2,1,0:T(8,128)}, bf16[2,4,111,4096]{3,2,1,0:T(8,128)(2,1)}, f32[16,4096]{1,0:T(8,128)}, s32[]{:T(128)}, ...), condition=%wide.region_1.2_spmd.clone, body=%wide.region_0.1_spmd.clone.sunk | while | flops 12582915 | bytes 31506524 | solution.py:57
  16.2 9.4 %select_add_fusion.2 = f32[2,4,96,4096]{3,2,1,0:T(8,128)} fusion(f32[2,4,96,4096]{3,2,1,0:T(8,128)} %get-tuple-element.146, f32[4096]{0:T(1024)S(1)} %bitcast.157, bf16[2,4,111,4096]{3,2,1,0:T(8,128)(2,1)} %get-tuple-element.153, s32[]{:T(128)S(6)} %copy.118, pred[]{:T(512)S(6)} %compare.11), kind=kLoop, calls=%fused_computation.clone.1 | loop fusion | flops 12582912 | bytes 31473668 | tf_op jit(solution)/shard_map/while/body/eval_jaxpr/add | solution.py:54
  26.5 13.1 %select_add_fusion.2 = f32[2,4,96,4096]{3,2,1,0:T(8,128)} fusion(f32[2,4,96,4096]{3,2,1,0:T(8,128)} %get-tuple-element.146, f32[4096]{0:T(1024)S(1)} %bitcast.157, bf16[2,4,111,4096]{3,2,1,0:T(8,128)(2,1)} %get-tuple-element.153, s32[]{:T(128)S(6)} %copy.118, pred[]{:T(512)S(6)} %compare.11), kind=kLoop, calls=%fused_computation.clone.1 | loop fusion | flops 12582912 | bytes 31473668 | tf_op jit(solution)/shard_map/while/body/eval_jaxpr/add | solution.py:54
  40.5 13.1 %select_add_fusion.2 = f32[2,4,96,4096]{3,2,1,0:T(8,128)} fusion(f32[2,4,96,4096]{3,2,1,0:T(8,128)} %get-tuple-element.146, f32[4096]{0:T(1024)S(1)} %bitcast.157, bf16[2,4,111,4096]{3,2,1,0:T(8,128)(2,1)} %get-tuple-element.153, s32[]{:T(128)S(6)} %copy.118, pred[]{:T(512)S(6)} %compare.11), kind=kLoop, calls=%fused_computation.clone.1 | loop fusion | flops 12582912 | bytes 31473668 | tf_op jit(solution)/shard_map/while/body/eval_jaxpr/add | solution.py:54
  54.6 13.1 %select_add_fusion.2 = f32[2,4,96,4096]{3,2,1,0:T(8,128)} fusion(f32[2,4,96,4096]{3,2,1,0:T(8,128)} %get-tuple-element.146, f32[4096]{0:T(1024)S(1)} %bitcast.157, bf16[2,4,111,4096]{3,2,1,0:T(8,128)(2,1)} %get-tuple-element.153, s32[]{:T(128)S(6)} %copy.118, pred[]{:T(512)S(6)} %compare.11), kind=kLoop, calls=%fused_computation.clone.1 | loop fusion | flops 12582912 | bytes 31473668 | tf_op jit(solution)/shard_map/while/body/eval_jaxpr/add | solution.py:54
  68.6 13.1 %select_add_fusion.2 = f32[2,4,96,4096]{3,2,1,0:T(8,128)} fusion(f32[2,4,96,4096]{3,2,1,0:T(8,128)} %get-tuple-element.146, f32[4096]{0:T(1024)S(1)} %bitcast.157, bf16[2,4,111,4096]{3,2,1,0:T(8,128)(2,1)} %get-tuple-element.153, s32[]{:T(128)S(6)} %copy.118, pred[]{:T(512)S(6)} %compare.11), kind=kLoop, calls=%fused_computation.clone.1 | loop fusion | flops 12582912 | bytes 31473668 | tf_op jit(solution)/shard_map/while/body/eval_jaxpr/add | solution.py:54
  82.6 13.1 %select_add_fusion.2 = f32[2,4,96,4096]{3,2,1,0:T(8,128)} fusion(f32[2,4,96,4096]{3,2,1,0:T(8,128)} %get-tuple-element.146, f32[4096]{0:T(1024)S(1)} %bitcast.157, bf16[2,4,111,4096]{3,2,1,0:T(8,128)(2,1)} %get-tuple-element.153, s32[]{:T(128)S(6)} %copy.118, pred[]{:T(512)S(6)} %compare.11), kind=kLoop, calls=%fused_computation.clone.1 | loop fusion | flops 12582912 | bytes 31473668 | tf_op jit(solution)/shard_map/while/body/eval_jaxpr/add | solution.py:54
  96.6 13.1 %select_add_fusion.2 = f32[2,4,96,4096]{3,2,1,0:T(8,128)} fusion(f32[2,4,96,4096]{3,2,1,0:T(8,128)} %get-tuple-element.146, f32[4096]{0:T(1024)S(1)} %bitcast.157, bf16[2,4,111,4096]{3,2,1,0:T(8,128)(2,1)} %get-tuple-element.153, s32[]{:T(128)S(6)} %copy.118, pred[]{:T(512)S(6)} %compare.11), kind=kLoop, calls=%fused_computation.clone.1 | loop fusion | flops 12582912 | bytes 31473668 | tf_op jit(solution)/shard_map/while/body/eval_jaxpr/add | solution.py:54
  110.6 13.1 %select_add_fusion.2 = f32[2,4,96,4096]{3,2,1,0:T(8,128)} fusion(f32[2,4,96,4096]{3,2,1,0:T(8,128)} %get-tuple-element.146, f32[4096]{0:T(1024)S(1)} %bitcast.157, bf16[2,4,111,4096]{3,2,1,0:T(8,128)(2,1)} %get-tuple-element.153, s32[]{:T(128)S(6)} %copy.118, pred[]{:T(512)S(6)} %compare.11), kind=kLoop, calls=%fused_computation.clone.1 | loop fusion | flops 12582912 | bytes 31473668 | tf_op jit(solution)/shard_map/while/body/eval_jaxpr/add | solution.py:54
  124.6 13.1 %select_add_fusion.2 = f32[2,4,96,4096]{3,2,1,0:T(8,128)} fusion(f32[2,4,96,4096]{3,2,1,0:T(8,128)} %get-tuple-element.146, f32[4096]{0:T(1024)S(1)} %bitcast.157, bf16[2,4,111,4096]{3,2,1,0:T(8,128)(2,1)} %get-tuple-element.153, s32[]{:T(128)S(6)} %copy.118, pred[]{:T(512)S(6)} %compare.11), kind=kLoop, calls=%fused_computation.clone.1 | loop fusion | flops 12582912 | bytes 31473668 | tf_op jit(solution)/shard_map/while/body/eval_jaxpr/add | solution.py:54
  138.6 13.1 %select_add_fusion.2 = f32[2,4,96,4096]{3,2,1,0:T(8,128)} fusion(f32[2,4,96,4096]{3,2,1,0:T(8,128)} %get-tuple-element.146, f32[4096]{0:T(1024)S(1)} %bitcast.157, bf16[2,4,111,4096]{3,2,1,0:T(8,128)(2,1)} %get-tuple-element.153, s32[]{:T(128)S(6)} %copy.118, pred[]{:T(512)S(6)} %compare.11), kind=kLoop, calls=%fused_computation.clone.1 | loop fusion | flops 12582912 | bytes 31473668 | tf_op jit(solution)/shard_map/while/body/eval_jaxpr/add | solution.py:54
  152.7 13.1 %select_add_fusion.2 = f32[2,4,96,4096]{3,2,1,0:T(8,128)} fusion(f32[2,4,96,4096]{3,2,1,0:T(8,128)} %get-tuple-element.146, f32[4096]{0:T(1024)S(1)} %bitcast.157, bf16[2,4,111,4096]{3,2,1,0:T(8,128)(2,1)} %get-tuple-element.153, s32[]{:T(128)S(6)} %copy.118, pred[]{:T(512)S(6)} %compare.11), kind=kLoop, calls=%fused_computation.clone.1 | loop fusion | flops 12582912 | bytes 31473668 | tf_op jit(solution)/shard_map/while/body/eval_jaxpr/add | solution.py:54
  166.7 13.1 %select_add_fusion.2 = f32[2,4,96,4096]{3,2,1,0:T(8,128)} fusion(f32[2,4,96,4096]{3,2,1,0:T(8,128)} %get-tuple-element.146, f32[4096]{0:T(1024)S(1)} %bitcast.157, bf16[2,4,111,4096]{3,2,1,0:T(8,128)(2,1)} %get-tuple-element.153, s32[]{:T(128)S(6)} %copy.118, pred[]{:T(512)S(6)} %compare.11), kind=kLoop, calls=%fused_computation.clone.1 | loop fusion | flops 12582912 | bytes 31473668 | tf_op jit(solution)/shard_map/while/body/eval_jaxpr/add | solution.py:54
  180.7 13.1 %select_add_fusion.2 = f32[2,4,96,4096]{3,2,1,0:T(8,128)} fusion(f32[2,4,96,4096]{3,2,1,0:T(8,128)} %get-tuple-element.146, f32[4096]{0:T(1024)S(1)} %bitcast.157, bf16[2,4,111,4096]{3,2,1,0:T(8,128)(2,1)} %get-tuple-element.153, s32[]{:T(128)S(6)} %copy.118, pred[]{:T(512)S(6)} %compare.11), kind=kLoop, calls=%fused_computation.clone.1 | loop fusion | flops 12582912 | bytes 31473668 | tf_op jit(solution)/shard_map/while/body/eval_jaxpr/add | solution.py:54
  194.7 13.1 %select_add_fusion.2 = f32[2,4,96,4096]{3,2,1,0:T(8,128)} fusion(f32[2,4,96,4096]{3,2,1,0:T(8,128)} %get-tuple-element.146, f32[4096]{0:T(1024)S(1)} %bitcast.157, bf16[2,4,111,4096]{3,2,1,0:T(8,128)(2,1)} %get-tuple-element.153, s32[]{:T(128)S(6)} %copy.118, pred[]{:T(512)S(6)} %compare.11), kind=kLoop, calls=%fused_computation.clone.1 | loop fusion | flops 12582912 | bytes 31473668 | tf_op jit(solution)/shard_map/while/body/eval_jaxpr/add | solution.py:54
  208.7 13.1 %select_add_fusion.2 = f32[2,4,96,4096]{3,2,1,0:T(8,128)} fusion(f32[2,4,96,4096]{3,2,1,0:T(8,128)} %get-tuple-element.146, f32[4096]{0:T(1024)S(1)} %bitcast.157, bf16[2,4,111,4096]{3,2,1,0:T(8,128)(2,1)} %get-tuple-element.153, s32[]{:T(128)S(6)} %copy.118, pred[]{:T(512)S(6)} %compare.11), kind=kLoop, calls=%fused_computation.clone.1 | loop fusion | flops 12582912 | bytes 31473668 | tf_op jit(solution)/shard_map/while/body/eval_jaxpr/add | solution.py:54
  222.7 13.1 %select_add_fusion.2 = f32[2,4,96,4096]{3,2,1,0:T(8,128)} fusion(f32[2,4,96,4096]{3,2,1,0:T(8,128)} %get-tuple-element.146, f32[4096]{0:T(1024)S(1)} %bitcast.157, bf16[2,4,111,4096]{3,2,1,0:T(8,128)(2,1)} %get-tuple-element.153, s32[]{:T(128)S(6)} %copy.118, pred[]{:T(512)S(6)} %compare.11), kind=kLoop, calls=%fused_computation.clone.1 | loop fusion | flops 12582912 | bytes 31473668 | tf_op jit(solution)/shard_map/while/body/eval_jaxpr/add | solution.py:54
  235.8 15.6 %copy.44 = f32[2,4,96,4096]{2,3,1,0:T(8,128)} copy(f32[2,4,96,4096]{3,2,1,0:T(8,128)} %get-tuple-element.84) | data formatting | bytes 25165824 | tf_op jit(solution)/shard_map/while | solution.py:57
  251.4 9.9 %fusion.125 = (f32[1,4,96,4096]{2,3,1,0:T(8,128)S(1)}, f32[1,4,96,4096]{2,3,1,0:T(8,128)}) fusion(f32[2,4,96,4096]{2,3,1,0:T(8,128)} %copy.44), kind=kLoop, calls=%fused_computation.136 | loop fusion | bytes 25165824 | tf_op jit(solution)/shard_map/slice | solution.py:59
  261.3 13.3 %fusion.12 = f32[4,96,64,64]{1,3,2,0:T(8,128)} fusion(f32[4,96,64,64]{1,3,2,0:T(8,128)S(1)} %bitcast.147), kind=kOutput, calls=%fused_computation.16 | convolution fusion | flops 1208016896 | bytes 12582912 | tf_op jit(solution)/shard_map/lsab,ak->lsbk/dot_general | solution.py:66
  274.6 13.5 %fusion.14 = f32[4,96,64,64]{1,3,2,0:T(8,128)} fusion(f32[4,96,64,64]{1,3,2,0:T(8,128)S(1)} %bitcast.148), kind=kOutput, calls=%fused_computation.18 | convolution fusion | flops 1208016896 | bytes 12582912 | tf_op jit(solution)/shard_map/lsab,ak->lsbk/dot_general | solution.py:66
  288.2 18.1 %fusion.10 = f32[4,96,64,64]{1,3,2,0:T(8,128)} fusion(f32[4,96,64,64]{1,3,2,0:T(8,128)} %bitcast.149), kind=kOutput, calls=%fused_computation.14 | convolution fusion | flops 1208016896 | bytes 12582912 | tf_op jit(solution)/shard_map/lsab,ak->lsbk/dot_general | solution.py:66
  306.2 25.9 %multiply_add_fusion = (f32[4,96,64,64]{1,3,2,0:T(8,128)}, f32[4,96,64,64]{1,3,2,0:T(8,128)}) fusion(f32[64,64]{1,0:T(8,128)S(1)} %copy.51, f32[64,64]{1,0:T(8,128)S(1)} %copy.48, f32[4,96,64,64]{1,3,2,0:T(8,128)} %fusion.12, f32[4,96,64,64]{1,3,2,0:T(8,128)} %fusion.14, f32[4,96,64,64]{1,3,2,0:T(8,128)} %fusion.10, f32[4,96,64,64]{1,3,2,0:T(8,128)} %bitcast.150), kind=kOutput, calls=%fused_computation.3 | convolution fusion | flops 1220599808 | bytes 37781504 | tf_op jit(solution)/shard_map/lsab,ak->lsbk/dot_general | solution.py:66
  332.2 13.5 %fusion = f32[4,4,96,64]{2,0,3,1:T(4,128)S(1)} fusion(f32[4,96,64,64]{1,3,2,0:T(8,128)} %get-tuple-element.109), kind=kOutput, calls=%fused_computation.4 | convolution fusion | flops 75501056 | bytes 6684672 | tf_op jit(solution)/shard_map/lsbk,bj->jkls/dot_general | solution.py:78
  345.7 8.6 %fusion.2 = f32[4,4,96,64]{2,0,3,1:T(4,128)S(1)} fusion(f32[4,96,64,64]{1,3,2,0:T(8,128)S(1)} %copy-done), kind=kOutput, calls=%fused_computation.6 | convolution fusion | flops 75501056 | bytes 6684672 | tf_op jit(solution)/shard_map/lsbk,bj->jkls/dot_general | solution.py:78
  354.3 8.8 %fusion.27 = f32[4,64,4,96]{3,0,1,2:T(4,128)S(1)} fusion(f32[4,4,96,64]{2,0,3,1:T(4,128)S(1)} %fusion, f32[4,96,64,64]{1,3,2,0:T(8,128)S(1)} %bitcast.152), kind=kOutput, calls=%fused_computation.27 | convolution fusion | flops 75697664 | bytes 7077888 | tf_op jit(solution)/shard_map/lsbk,bj->jkls/dot_general | solution.py:78
  363.1 8.8 %fusion.33 = f32[4,64,4,96]{3,0,1,2:T(4,128)S(1)} fusion(f32[4,4,96,64]{2,0,3,1:T(4,128)S(1)} %fusion.2, f32[4,96,64,64]{1,3,2,0:T(8,128)S(1)} %bitcast.152), kind=kOutput, calls=%fused_computation.29 | convolution fusion | flops 75697664 | bytes 7077888 | tf_op jit(solution)/shard_map/lsbk,bj->jkls/dot_general | solution.py:78
  373.6 37.8 %all-gather.3.cloned.1.call-done = f32[256,8,192]{0,2,1:T(8,128)} async-done(((f32[256,4,192]{0,2,1:T(8,128)}), f32[256,8,192]{0,2,1:T(8,128)}) %all-gather.3.cloned.1.call-update) | async-done | bytes 1572880 | tf_op jit(solution)/shard_map/all_gather | solution.py:88
  414.3 11.5 %all-to-all-start = ((f32[256,2,4,192]{3,2,1,0:T(4,128)}), f32[256,2,4,192]{3,2,1,0:T(4,128)S(1)}, u32[]{:S(2)}, u32[]{:S(2)}) async-start(f32[256,2,4,192]{3,2,1,0:T(4,128)} %copy.59), calls=%async_computation | async-start | bytes 4194304 | tf_op jit(solution)/shard_map/all_to_all | solution.py:89
  425.8 50.2 %all-to-all-done = f32[256,2,4,192]{3,2,1,0:T(4,128)S(1)} async-done(((f32[256,2,4,192]{3,2,1,0:T(4,128)}), f32[256,2,4,192]{3,2,1,0:T(4,128)S(1)}, u32[]{:S(2)}, u32[]{:S(2)}) %all-to-all-start) | async-done | bytes 1572896 | tf_op jit(solution)/shard_map/all_to_all | solution.py:89
  496.4 6.2 %copy.69 = bf16[2,8,256,512]{3,2,1,0:T(8,128)(2,1)} copy(bf16[2,8,256,512]{2,3,0,1:T(8,128)(2,1)} %fusion.53) | data formatting | bytes 8388608 | tf_op jit(solution)/shard_map/stack | solution.py:31
  (52 shorter events, 40.1 us)
Async XLA Ops:
  6.5 404.9 %all-gather.3.cloned.1.call-start = ((), (), s32[]{:S(2)}) async-start(), calls=%async_computation.1 | async-start | bytes 2359296 | tf_op jit(solution)/shard_map/all_gather | solution.py:88
  332.2 13.5 %copy-start = (f32[4,96,64,64]{1,3,2,0:T(8,128)S(1)}, f32[4,96,64,64]{1,3,2,0:T(8,128)}, u32[]{:S(2)}) copy-start(f32[4,96,64,64]{1,3,2,0:T(8,128)} %get-tuple-element.109) | copy-start | bytes 18874372
  332.2 22.1 %slice-start = ((s8[8388608]{0:T(1024)(128)(4,1)}), s8[4194304]{0:T(1024)(128)(4,1)S(1)}, s32[]{:S(2)}) async-start(s8[8388608]{0:T(1024)(128)(4,1)} %bitcast.151), calls=%async_computation.2 | async-start | bytes 8388608
  345.6 8.6 %slice-start.1 = ((s8[8388608]{0:T(1024)(128)(4,1)}), s8[4194304]{0:T(1024)(128)(4,1)S(1)}, s32[]{:S(2)}) async-start(s8[8388608]{0:T(1024)(128)(4,1)} %bitcast.151), calls=%async_computation.3 | async-start | bytes 8388608
  372.0 53.8 %copy-start.1 = (s32[512,2]{0,1:T(2,128)S(1)}, s32[512,2]{0,1:T(2,128)}, u32[]{:S(2)}) copy-start(s32[512,2]{0,1:T(2,128)} %param.7) | copy-start | bytes 12292
  414.3 61.7 %all-to-all-start = ((f32[256,2,4,192]{3,2,1,0:T(4,128)}), f32[256,2,4,192]{3,2,1,0:T(4,128)S(1)}, u32[]{:S(2)}, u32[]{:S(2)}) async-start(f32[256,2,4,192]{3,2,1,0:T(4,128)} %copy.59), calls=%async_computation | async-start | bytes 4194304 | tf_op jit(solution)/shard_map/all_to_all | solution.py:89
Sparse Core Ops, SparseCore 0:
  373.7 37.6 all-gather.2
where the time goes:
time: 519 us; the launch traced here: 510 us
  other arithmetic  214 us (41%)
  matrix products  118 us (23%)
  waiting for transfers between devices  88 us (17%)
  local copies, waits for them, and re-layouts  64.2 us (12%)
  between operations  13.9 us (3%)
  starting transfers between devices  11.5 us (2%)
    add x16, other arithmetic, add_tap(): return total + window * weight  206 us
    dot_general x4, matrix products, section_one(): return jnp.einsum('lsab,ak->lsbk', data, table, precision=highest)  70.7 us
    all_to_all x1, waiting for transfers between devices, on_device(): lax.all_to_all(paired, 'chan', split_axis=0, concat_axis=2, tiled=True)  50.2 us
    dot_general x4, matrix products, section_two(): return jnp.einsum('lsbk,bj->jkls', data, table, precision=highest)  39.7 us
    all_gather x1, waiting for transfers between devices, on_device(): paired = lax.all_gather(moved[:, None], 'tile', axis=1, tiled=True)  37.8 us
    while x1, local copies, waits for them, and re-layouts, on_device(): filtered = lax.fori_loop(0, tap_count, add_tap, start_sum)  15.6 us
    dynamic_slice x16, local copies, waits for them, and re-layouts, add_tap(): weight = lax.dynamic_index_in_dim(filter_taps, tap_index, 0, keepdims=False)  14.7 us
    all_to_all x1, starting transfers between devices, on_device(): lax.all_to_all(paired, 'chan', split_axis=0, concat_axis=2, tiled=True)  11.5 us
  transfers between devices with their start and end apart: 2, of which 2 were waited for; matrix products, arithmetic and copies ran while one was open for 0% of the time, Pallas kernels for 0%

commit v1 on v0

v1 whole, which is shorter than its diff:
```python
import functools
import math

import jax
import jax.numpy as jnp
import numpy as np
from jax import lax
from jax.experimental import pallas as pl
from jax.experimental.pallas import tpu as pltpu
from jax.sharding import PartitionSpec as P

STATIONS_HERE = 4
CHUNKS = 2
SPECTRA = 96
PART = SPECTRA // CHUNKS
TAPS = 16
FRAMES = SPECTRA + TAPS - 1
NCHAN = 4096
LANES = 128
STEPS = 4
OWNERS = 128
WORD = 2 * PART
ROWS = 2 * STATIONS_HERE * WORD // LANES
VMEM = 56 * 1024 * 1024


@functools.lru_cache(maxsize=None)
def transform_table():
    sample = np.arange(NCHAN // 2).reshape(STEPS, 1, -1, 1)
    channel = 2 * np.arange(OWNERS).reshape(1, 1, 1, -1) + np.arange(2).reshape(1, 2, 1, 1)
    angle = 2.0 * np.pi / NCHAN * (sample * channel % NCHAN)
    table = np.concatenate((np.cos(angle), np.sin(angle)), axis=-1) / math.sqrt(NCHAN)
    high = table.astype(np.float32).astype(jnp.bfloat16)
    low = (table - high.astype(np.float64)).astype(np.float32).astype(jnp.bfloat16)
    return np.stack((high, low), axis=2)


def halves(value):
    high = value.astype(jnp.bfloat16)
    low = (value - high.astype(jnp.float32)).astype(jnp.bfloat16)
    return high, low


def channelise_kernel(first, good_ref, lower_ref, upper_ref, taps_ref, table_ref, out_ref, wide, filtered, total):
    step = pl.program_id(0)
    span = PART + TAPS - 1

    for side, samples in enumerate((lower_ref, upper_ref)):
        tap_ref = taps_ref.at[side]

        def column(index, carry, samples=samples, tap_ref=tap_ref, side=side):
            wide[...] = samples[index, first : first + span].astype(jnp.float32)
            for pair in range(2):
                weights = []
                for tap in range(TAPS):
                    at = 2 * pair * LANES
                    weights.append(
                        jnp.concatenate(
                            (
                                jnp.broadcast_to(tap_ref[tap : tap + 1, at : at + LANES], (4, LANES)),
                                jnp.broadcast_to(tap_ref[tap : tap + 1, at + LANES : at + 2 * LANES], (4, LANES)),
                            ),
                            axis=0,
                        )
                    )
                base = ((side * 2 + index) * 16 + pair * 8) * PART
                sums = {}
                for frame in range(span):
                    sample = wide[frame, 8 * pair : 8 * pair + 8, :]
                    for tap in range(TAPS):
                        spectrum = frame - tap
                        if 0 <= spectrum < PART:
                            term = sample * weights[tap]
                            sums[spectrum] = term if tap == 0 else sums[spectrum] + term
                    done = frame - TAPS + 1
                    if done >= 0:
                        filtered[pl.ds(base + done, 8, stride=PART), :] = sums.pop(done)
            return carry

        lax.fori_loop(0, 2, column, 0)

    rows = STATIONS_HERE * PART

    def block(side, part, line):
        return filtered[pl.ds(((side * 2 + part) * 16 + 4 * line) * PART, rows), :]

    for parity in range(2):
        for part in range(2):
            high, low = [], []
            for line in range(4):
                one, two = block(0, part, line), block(1, part, line)
                h, l = halves(one + two if parity == 0 else one - two)
                high.append(h)
                low.append(l)
            high = jnp.concatenate(high, axis=1)
            low = jnp.concatenate(low, axis=1)
            dot = functools.partial(jnp.dot, preferred_element_type=jnp.float32)
            product = (
                dot(high, table_ref[0, parity, 0])
                + dot(low, table_ref[0, parity, 0])
                + dot(high, table_ref[0, parity, 1])
            )

            @pl.when(step == 0)
            def _(parity=parity, part=part, product=product):
                total[parity, part] = product

            @pl.when(step > 0)
            def _(parity=parity, part=part, product=product):
                total[parity, part] += product

    @pl.when(step == STEPS - 1)
    def _():
        for parity in range(2):
            real = total[parity, 0, :, :LANES] + total[parity, 1, :, LANES:]
            imag = total[parity, 1, :, :LANES] - total[parity, 0, :, LANES:]
            word = []
            for station in range(STATIONS_HERE):
                mask = good_ref[station].astype(jnp.float32)
                at = slice(station * PART, (station + 1) * PART)
                word.append(jnp.concatenate((real[at], imag[at]), axis=0) * mask)
            for row in range(3):
                tile = jnp.concatenate((word[row], word[3][32 * row : 32 * row + 32]), axis=0)
                out_ref[pl.ds(parity * 3 + row, OWNERS, stride=ROWS), :] = tile.T


def channelise(first, good, samples, taps, table):
    return pl.pallas_call(
        functools.partial(channelise_kernel, first),
        grid=(STEPS,),
        in_specs=[
            pl.BlockSpec(memory_space=pltpu.SMEM),
            pl.BlockSpec((2, FRAMES, 16, LANES), lambda q: (0, 0, q, 0)),
            pl.BlockSpec((2, FRAMES, 16, LANES), lambda q: (0, 0, q + STEPS, 0)),
            pl.BlockSpec((2, TAPS, 4 * LANES), lambda q: (0, 0, q)),
            pl.BlockSpec((1, 2, 2, 4 * LANES, 2 * OWNERS), lambda q: (q, 0, 0, 0, 0)),
        ],
        out_specs=pl.BlockSpec((OWNERS * ROWS, LANES), lambda q: (0, 0)),
        out_shape=jax.ShapeDtypeStruct((OWNERS * ROWS, LANES), jnp.float32),
        scratch_shapes=[
            pltpu.VMEM((PART + TAPS - 1, 16, LANES), jnp.float32),
            pltpu.VMEM((2 * 2 * 16 * PART, LANES), jnp.float32),
            pltpu.VMEM((2, 2, STATIONS_HERE * PART, 2 * OWNERS), jnp.float32),
        ],
        compiler_params=pltpu.CompilerParams(vmem_limit_bytes=VMEM),
        cost_estimate=pl.CostEstimate(flops=3_000_000_000, bytes_accessed=12_000_000, transcendentals=0),
        name="channelise",
    )(good, samples, samples, taps, table)


def correlate_kernel(side_ref, own0, own1, other0, other1, out_ref, stations, high, low, turned_high, turned_low):
    parity, section = pl.program_id(0), pl.program_id(1)
    side = side_ref[0]
    lane = lax.broadcasted_iota(jnp.int32, (OWNERS, LANES), 1)

    @pl.when(section == 0)
    def _():
        for which, pair in enumerate(((own0, own1), (other0, other1))):
            slot = side if which == 0 else 1 - side
            for chunk, ref in enumerate(pair):
                rows = [ref[pl.ds(parity * 3 + row, OWNERS, stride=ROWS), :] for row in range(3)]
                for station in range(3):
                    stations[pl.ds(station, OWNERS, stride=4), :] = jnp.where(lane < WORD, rows[station], 0.0)
                last = jnp.where(
                    lane < 32,
                    pltpu.roll(rows[0], 32, 1),
                    jnp.where(lane < 64, pltpu.roll(rows[1], 64, 1), pltpu.roll(rows[2], 96, 1)),
                )
                stations[pl.ds(3, OWNERS, stride=4), :] = jnp.where(lane < WORD, last, 0.0)
                at = slice(chunk * LANES, (chunk + 1) * LANES)
                h, l = halves(stations[...])
                high[slot, :, at] = h
                low[slot, :, at] = l
                mine = stations[pl.ds(pl.multiple_of(side * 256, 256), 256), :]
                column = lax.broadcasted_iota(jnp.int32, (256, LANES), 1)
                turned = jnp.where(
                    column < PART,
                    pltpu.roll(mine, LANES - PART, 1),
                    jnp.where(column < WORD, -pltpu.roll(mine, PART, 1), 0.0),
                )
                h, l = halves(turned)
                turned_high[slot, :, at] = h
                turned_low[slot, :, at] = l

    def product(a_high, a_low, b_high, b_low):
        dot = lambda a, b: lax.dot_general(a, b, (((1,), (1,)), ((), ())), preferred_element_type=jnp.float32)
        return (dot(a_high, b_high) + dot(a_low, b_high) + dot(a_high, b_low)) * (1.0 / SPECTRA)

    first = pl.ds(pl.multiple_of(side * 256 + section * 128, 128), 128)
    local = pl.ds(pl.multiple_of(section * 128, 128), 128)
    real = [[product(high[p, first, :], low[p, first, :], high[q], low[q]) for q in range(2)] for p in range(2)]
    imag = [[product(turned_high[p, local, :], turned_low[p, local, :], high[q], low[q]) for q in range(2)] for p in range(2)]
    planes = (
        real[0][0] + real[1][1],
        real[0][0] - real[1][1],
        real[0][1] + real[1][0],
        imag[0][1] - imag[1][0],
        imag[0][0] + imag[1][1],
        imag[0][0] - imag[1][1],
        imag[0][1] + imag[1][0],
        real[1][0] - real[0][1],
    )
    for index, plane in enumerate(planes):
        out_ref[0, index] = plane.astype(jnp.bfloat16)


def correlate(side, own0, own1, other0, other1):
    whole = pl.BlockSpec((OWNERS * ROWS, LANES), lambda c, a: (0, 0))
    return pl.pallas_call(
        correlate_kernel,
        grid=(2, 2),
        in_specs=[pl.BlockSpec(memory_space=pltpu.SMEM), whole, whole, whole, whole],
        out_specs=pl.BlockSpec((1, 8, 128, 512), lambda c, a: (c, 0, a, 0)),
        out_shape=jax.ShapeDtypeStruct((2, 8, 256, 512), jnp.bfloat16),
        scratch_shapes=[
            pltpu.VMEM((512, LANES), jnp.float32),
            pltpu.VMEM((2, 512, 2 * LANES), jnp.bfloat16),
            pltpu.VMEM((2, 512, 2 * LANES), jnp.bfloat16),
            pltpu.VMEM((2, 256, 2 * LANES), jnp.bfloat16),
            pltpu.VMEM((2, 256, 2 * LANES), jnp.bfloat16),
        ],
        compiler_params=pltpu.CompilerParams(vmem_limit_bytes=VMEM),
        cost_estimate=pl.CostEstimate(flops=3_300_000_000, bytes_accessed=8_000_000, transcendentals=0),
        name="correlate",
    )(side, own0, own1, other0, other1)


def on_device(voltages, filter_taps, input_good):
    table = jnp.asarray(transform_table())
    chan, tile = lax.axis_index("chan"), lax.axis_index("tile")
    samples = voltages.reshape(2, STATIONS_HERE, FRAMES, NCHAN // LANES, LANES)
    samples = samples.transpose(0, 2, 3, 1, 4).reshape(2, FRAMES, LANES, LANES)
    taps = jnp.stack((filter_taps[:, : NCHAN // 2], filter_taps[:, NCHAN // 2 :]))
    good = lax.dynamic_slice(input_good, (chan * STATIONS_HERE, tile), (STATIONS_HERE, 1)).reshape(STATIONS_HERE)
    own, other = [], []
    for chunk in range(CHUNKS):
        spectra = channelise(chunk * PART, good, samples, taps, table)
        spectra = spectra.reshape(OWNERS, 1, ROWS * LANES)
        joined = lax.all_to_all(spectra, "chan", split_axis=0, concat_axis=0, tiled=True)
        joined = joined.reshape(OWNERS * ROWS, LANES)
        own.append(joined)
        other.append(lax.ppermute(joined, "tile", ((0, 1), (1, 0))))
    return correlate(tile.reshape(1).astype(jnp.int32), own[0], own[1], other[0], other[1])


def solution(mesh):
    in_specs = (P(None, "chan", "tile", None), P(), P())
    out_specs = P("chan", None, "tile", None)
    return jax.shard_map(on_device, mesh=mesh, in_specs=in_specs, out_specs=out_specs, check_vma=False)
```

time: 519 us -> 106 us (0.20); the launches traced: 510 us -> 105 us
  other arithmetic: 214 us -> 0.72 us
  matrix products: 118 us -> 0 us
  waiting for transfers between devices: 88 us -> 20.9 us
  local copies, waits for them, and re-layouts: 64.2 us -> 2.42 us
  Pallas kernels: 0 us -> 48.5 us
  starting transfers between devices: 11.5 us -> 32.4 us
  between operations: 13.9 us -> 0.04 us
    add x16 -> x0, other arithmetic: 206 us -> none  [add_tap(): return total + window * weight]
    dot_general x10 -> x0, matrix products: 118 us -> none  [the longest x4 70.7 us: section_one(): return jnp.einsum('lsab,ak->lsbk', data, table, precision=highest)]
    pallas_call x0 -> x3, Pallas kernels: none -> 48.5 us  [the longest x2 35.1 us: channelise(): pl.pallas_call(functools.partial(channelise_kernel, first), grid=(STEPS,)...]
    all_gather x1 -> x0, waiting for transfers between devices: 37.8 us -> none  [on_device(): paired = lax.all_gather(moved[:, None], 'tile', axis=1, tiled=True)]
    all_to_all x1 -> x2, waiting for transfers between devices: 50.2 us -> 13.4 us  [on_device(): lax.all_to_all(spectra, 'chan', split_axis=0, concat_axis=0, tiled=True)]
    while x1 -> x0, local copies, waits for them, and re-layouts: 15.6 us -> none  [on_device(): filtered = lax.fori_loop(0, tap_count, add_tap, start_sum)]
    all_to_all x1 -> x2, starting transfers between devices: 11.5 us -> 27 us  [on_device(): lax.all_to_all(spectra, 'chan', split_axis=0, concat_axis=0, tiled=True)]
    dynamic_slice x16 -> x0, local copies, waits for them, and re-layouts: 14.7 us -> none  [add_tap(): weight = lax.dynamic_index_in_dim(filter_taps, tap_index, 0, keepdims=False)]
  transfers between devices with their start and end apart: 2 -> 4, of which waited for: 2 -> 2; matrix products, arithmetic and copies ran while one was open for 0% -> 0% of each run, Pallas kernels for 0% -> 17%
where the time goes in v1:
time: 106 us; the launch traced here: 105 us
  Pallas kernels  48.5 us (46%)
  starting transfers between devices  32.4 us (31%)
  waiting for transfers between devices  20.9 us (20%)
  local copies, waits for them, and re-layouts  2.42 us (2%)
    pallas_call x2, Pallas kernels, channelise(): pl.pallas_call(functools.partial(channelise_kernel, first), grid=(STEPS,)...  35.1 us
    all_to_all x2, starting transfers between devices, on_device(): lax.all_to_all(spectra, 'chan', split_axis=0, concat_axis=0, tiled=True)  27 us
    all_to_all x2, waiting for transfers between devices, on_device(): lax.all_to_all(spectra, 'chan', split_axis=0, concat_axis=0, tiled=True)  13.4 us
    pallas_call x1, Pallas kernels, correlate(): pl.pallas_call(correlate_kernel, grid=(2, 2), in_specs=[pl.BlockSpec(memo...  13.3 us
    ppermute x2, waiting for transfers between devices, on_device(): other.append(lax.ppermute(joined, 'tile', ((0, 1), (1, 0))))  7.46 us
    ppermute x2, starting transfers between devices, on_device(): other.append(lax.ppermute(joined, 'tile', ((0, 1), (1, 0))))  5.33 us
  transfers between devices with their start and end apart: 4, of which 2 were waited for; matrix products, arithmetic and copies ran while one was open for 0% of the time, Pallas kernels for 17%

profile of v1, /device:TPU:1, one launch (start us, length us, event | category | flops | bytes accessed | tf_op | source)
XLA Modules:
  0.0 104.9 jit_solution(678671724648306638)
XLA Ops:
  0.0 0.0 copy-start
  0.0 1.0 slice_bitcast_fusion.1
  1.0 0.7 pad_maximum_fusion.taps_ref
  1.7 0.0 copy-done
  1.7 0.6 dynamic-slice_bitcast_fusion.good_ref
  2.4 17.5 %channelise.2 = f32[768,128]{1,0:T(8,128)} custom-call(s32[4]{0:T(128)} %dynamic-slice_bitcast_fusion.good_ref, bf16[2,111,128,128]{3,2,1,0:T(8,128)(2,1)} %bitcast.16, bf16[2,111,128,128]{3,2,1,0:T(8,128)(2,1)} %bitcast.17, f32[2,16,2048]{2,1,0:T(8,128)} %pad_maximum_fusion.taps_ref, bf16[4,2,2,512,256]{4,3,2,1,0:T(8,128)(2,1)} %constant.18.clone.table_ref), custom_call_target="tpu_custom_call" | custom-call | flops 3000000000 | bytes 12000000 | tf_op jit(solution)/shard_map/channelise/pallas_call | solution.py:128
  19.9 14.8 %all-to-all-start = ((f32[128,1,768]{2,1,0:T(1,128)}), f32[128,1,768]{2,1,0:T(1,128)S(1)}, u32[]{:S(2)}, u32[]{:S(2)}) async-start(f32[128,1,768]{2,1,0:T(1,128)} %bitcast.21), calls=%async_computation | async-start | bytes 786432 | tf_op jit(solution)/shard_map/all_to_all | solution.py:239
  34.7 17.6 %channelise.3 = f32[768,128]{1,0:T(8,128)} custom-call(s32[4]{0:T(128)} %dynamic-slice_bitcast_fusion.good_ref, bf16[2,111,128,128]{3,2,1,0:T(8,128)(2,1)} %bitcast.18, bf16[2,111,128,128]{3,2,1,0:T(8,128)(2,1)} %bitcast.19, f32[2,16,2048]{2,1,0:T(8,128)} %pad_maximum_fusion.taps_ref, bf16[4,2,2,512,256]{4,3,2,1,0:T(8,128)(2,1)} %constant.18.clone.table_ref), custom_call_target="tpu_custom_call" | custom-call | flops 3000000000 | bytes 12000000 | tf_op jit(solution)/shard_map/channelise/pallas_call | solution.py:128
  52.3 0.0 all-to-all-done
  52.3 0.0 copy-start.1
  52.3 12.2 %all-to-all-start.1 = ((f32[128,1,768]{2,1,0:T(1,128)}), f32[128,1,768]{2,1,0:T(1,128)S(1)}, u32[]{:S(2)}, u32[]{:S(2)}) async-start(f32[128,1,768]{2,1,0:T(1,128)} %bitcast.20), calls=%async_computation.1 | async-start | bytes 786432 | tf_op jit(solution)/shard_map/all_to_all | solution.py:239
  64.6 2.7 %collective-permute-start = (f32[768,128]{1,0:T(8,128)S(1)}, f32[768,128]{1,0:T(8,128)S(1)}, u32[]{:S(2)}, u32[]{:S(2)}) collective-permute-start(f32[768,128]{1,0:T(8,128)S(1)} %bitcast.22), channel_id=1, source_target_pairs={{0,1},{1,0},{2,3},{3,2},{4,5},{5,4},{6,7},{7,6},{8,9},{9,8},{10,11... | collective-permute-start | bytes 1179656 | tf_op jit(solution)/shard_map/ppermute | solution.py:242
  67.3 13.4 %all-to-all-done.1 = f32[128,1,768]{2,1,0:T(1,128)S(1)} async-done(((f32[128,1,768]{2,1,0:T(1,128)}), f32[128,1,768]{2,1,0:T(1,128)S(1)}, u32[]{:S(2)}, u32[]{:S(2)}) %all-to-all-start.1) | async-done | bytes 393248 | tf_op jit(solution)/shard_map/all_to_all | solution.py:239
  80.7 0.0 copy-start.2
  80.7 2.6 %collective-permute-start.1 = (f32[768,128]{1,0:T(8,128)S(1)}, f32[768,128]{1,0:T(8,128)S(1)}, u32[]{:S(2)}, u32[]{:S(2)}) collective-permute-start(f32[768,128]{1,0:T(8,128)S(1)} %bitcast.24), channel_id=1, source_target_pairs={{0,1},{1,0},{2,3},{3,2},{4,5},{5,4},{6,7},{7,6},{8,9},{9,8},{10,11... | collective-permute-start | bytes 1179656 | tf_op jit(solution)/shard_map/ppermute | solution.py:242
  83.3 0.0 collective-permute-done.other0
  83.3 0.0 copy-start.3
  83.3 7.5 %collective-permute-done.1.other1 = f32[768,128]{1,0:T(8,128)S(1)} collective-permute-done((f32[768,128]{1,0:T(8,128)S(1)}, f32[768,128]{1,0:T(8,128)S(1)}, u32[]{:S(2)}, u32[]{:S(2)}) %collective-permute-start.1) | collective-permute-done | bytes 393248 | tf_op jit(solution)/shard_map/ppermute | solution.py:242
  90.8 0.0 copy-start.4
  90.8 0.0 copy-done.1
  90.8 0.0 copy-done.2
  90.8 0.0 copy-done.3
  90.8 0.8 copy-done.4
  91.6 13.3 %correlate.1 = bf16[2,8,256,512]{3,2,1,0:T(8,128)(2,1)} custom-call(s32[1]{0:T(128)} %bitcast.side_ref, f32[768,128]{1,0:T(8,128)} %bitcast.23, f32[768,128]{1,0:T(8,128)} %bitcast.25, f32[768,128]{1,0:T(8,128)} %copy-done.3, f32[768,128]{1,0:T(8,128)} %copy-done.4), custom_call_target="tpu_custom_call" | custom-call | flops 3300000000 | bytes 8000000 | tf_op jit(solution)/shard_map/correlate/pallas_call | solution.py:209
Async XLA Ops:
  0.0 1.7 %copy-start = (s32[512,2]{0,1:T(2,128)S(1)}, s32[512,2]{0,1:T(2,128)}, u32[]{:S(2)}) copy-start(s32[512,2]{0,1:T(2,128)} %param.6) | copy-start | bytes 12292
  19.9 32.4 %all-to-all-start = ((f32[128,1,768]{2,1,0:T(1,128)}), f32[128,1,768]{2,1,0:T(1,128)S(1)}, u32[]{:S(2)}, u32[]{:S(2)}) async-start(f32[128,1,768]{2,1,0:T(1,128)} %bitcast.21), calls=%async_computation | async-start | bytes 786432 | tf_op jit(solution)/shard_map/all_to_all | solution.py:239
  52.3 38.5 %copy-start.1 = (f32[128,1,768]{2,1,0:T(1,128)}, f32[128,1,768]{2,1,0:T(1,128)S(1)}, u32[]{:S(2)}) copy-start(f32[128,1,768]{2,1,0:T(1,128)S(1)} %all-to-all-done) | copy-start | bytes 1179652
  52.3 28.4 %all-to-all-start.1 = ((f32[128,1,768]{2,1,0:T(1,128)}), f32[128,1,768]{2,1,0:T(1,128)S(1)}, u32[]{:S(2)}, u32[]{:S(2)}) async-start(f32[128,1,768]{2,1,0:T(1,128)} %bitcast.20), calls=%async_computation.1 | async-start | bytes 786432 | tf_op jit(solution)/shard_map/all_to_all | solution.py:239
  64.6 18.8 %collective-permute-start = (f32[768,128]{1,0:T(8,128)S(1)}, f32[768,128]{1,0:T(8,128)S(1)}, u32[]{:S(2)}, u32[]{:S(2)}) collective-permute-start(f32[768,128]{1,0:T(8,128)S(1)} %bitcast.22), channel_id=1, source_target_pairs={{0,1},{1,0},{2,3},{3,2},{4,5},{5,4},{6,7},{7,6},{8,9},{9,8},{10,11... | collective-permute-start | bytes 1179656 | tf_op jit(solution)/shard_map/ppermute | solution.py:242
  80.7 10.1 %copy-start.2 = (f32[128,1,768]{2,1,0:T(1,128)}, f32[128,1,768]{2,1,0:T(1,128)S(1)}, u32[]{:S(2)}) copy-start(f32[128,1,768]{2,1,0:T(1,128)S(1)} %all-to-all-done.1) | copy-start | bytes 1179652
  80.7 10.1 %collective-permute-start.1 = (f32[768,128]{1,0:T(8,128)S(1)}, f32[768,128]{1,0:T(8,128)S(1)}, u32[]{:S(2)}, u32[]{:S(2)}) collective-permute-start(f32[768,128]{1,0:T(8,128)S(1)} %bitcast.24), channel_id=1, source_target_pairs={{0,1},{1,0},{2,3},{3,2},{4,5},{5,4},{6,7},{7,6},{8,9},{9,8},{10,11... | collective-permute-start | bytes 1179656 | tf_op jit(solution)/shard_map/ppermute | solution.py:242
  83.3 7.5 %copy-start.3 = (f32[768,128]{1,0:T(8,128)}, f32[768,128]{1,0:T(8,128)S(1)}, u32[]{:S(2)}) copy-start(f32[768,128]{1,0:T(8,128)S(1)} %collective-permute-done.other0) | copy-start | bytes 1179652
  90.8 0.8 copy-start.4

commit v2 on v1

v2 whole, which is shorter than its diff:
```python
import functools
import math

import jax
import jax.numpy as jnp
import numpy as np
from jax import lax
from jax.experimental import pallas as pl
from jax.experimental.pallas import tpu as pltpu
from jax.sharding import Mesh
from jax.sharding import PartitionSpec as P

STATIONS_HERE = 4
SPECTRA = 96
TAPS = 16
FRAMES = SPECTRA + TAPS - 1
NCHAN = 4096
LANES = 128
STEPS = 4
OWNERS = 128
PARTS = ((0, 64), (64, 32))
AXES = ("z", "x", "yl", "core", "yh")
GROUP = ("z", "x", "core")
PEERS = 64
VMEM = 56 * 1024 * 1024
SMALL_VMEM = 28 * 1024 * 1024


@functools.lru_cache(maxsize=None)
def transform_table():
    sample = np.arange(NCHAN // 2).reshape(STEPS, 1, -1, 1)
    owner = np.arange(OWNERS).reshape(OWNERS // 4, 2, 2).transpose(1, 0, 2)
    channel = 2 * owner.reshape(1, 1, 1, -1) + np.arange(2).reshape(1, 2, 1, 1)
    angle = 2.0 * np.pi / NCHAN * (sample * channel % NCHAN)
    table = np.concatenate((np.cos(angle), np.sin(angle)), axis=-1) / math.sqrt(NCHAN)
    high = table.astype(np.float32).astype(jnp.bfloat16)
    low = (table - high.astype(np.float64)).astype(np.float32).astype(jnp.bfloat16)
    return np.concatenate((high, high, low), axis=2)


def halves(value):
    high = value.astype(jnp.bfloat16)
    low = (value - high.astype(jnp.float32)).astype(jnp.bfloat16)
    return high, low


def channelise_kernel(first, count, good_ref, samples, lower_taps, upper_taps, table_ref, earlier, out_ref, wide, filtered, split, total):
    step = pl.program_id(0)
    rows = STATIONS_HERE * count
    span = count + TAPS - 1
    half = count // 16

    def filter_part(part):
        for side, tap_ref in enumerate((lower_taps, upper_taps)):
            wide[side] = samples[part, first : first + span, side].astype(jnp.float32)
            for pair in range(2):
                weights = []
                for tap in range(TAPS):
                    at = 2 * pair * LANES
                    weights.append(
                        jnp.concatenate(
                            (
                                jnp.broadcast_to(tap_ref[tap : tap + 1, at : at + LANES], (4, LANES)),
                                jnp.broadcast_to(tap_ref[tap : tap + 1, at + LANES : at + 2 * LANES], (4, LANES)),
                            ),
                            axis=0,
                        )
                    )
                base = part * (8 * rows) + (side * 4 + pair * 2) * rows
                sums = {}
                for frame in range(span):
                    sample = wide[side, frame, 8 * pair : 8 * pair + 8, :]
                    for tap in range(TAPS):
                        spectrum = frame - tap
                        if 0 <= spectrum < count:
                            term = sample * weights[tap]
                            sums[spectrum] = term if tap == 0 else sums[spectrum] + term
                    done = frame - TAPS + 1
                    if done >= 0:
                        filtered[pl.ds(base + done, 8, stride=count), :] = sums.pop(done)

    for part in range(2):

        @pl.when(step >= 0)
        def _(part=part):
            filter_part(part)

    for part in range(2):
        for line in range(4):
            start = (part * 8 + line) * rows
            one = filtered[start : start + rows, :]
            two = filtered[start + 4 * rows : start + 5 * rows, :]
            for parity, value in enumerate((one + two, one - two)):
                h, l = halves(value)
                for term, piece in enumerate((h, l, h)):
                    at = (4 * term + line) * LANES
                    split[parity, part * rows : (part + 1) * rows, at : at + LANES] = piece
    for parity in range(2):
        product = jnp.dot(split[parity], table_ref[0, parity], preferred_element_type=jnp.float32)

        @pl.when(step == 0)
        def _(parity=parity, product=product):
            total[parity] = product

        @pl.when(step > 0)
        def _(parity=parity, product=product):
            total[parity] += product

    @pl.when(step == STEPS - 1)
    def _():
        for parity in range(2):
            real = total[parity, :rows, :LANES] + total[parity, rows:, LANES:]
            imag = total[parity, rows:, :LANES] - total[parity, :rows, LANES:]
            words = []
            for station in range(STATIONS_HERE):
                mask = good_ref[station].astype(jnp.float32)
                at = slice(station * count, (station + 1) * count)
                words += [real[at] * mask, imag[at] * mask]
            words = jnp.concatenate(words, axis=0)
            for row in range(half):
                tile = words[row * LANES : (row + 1) * LANES].T
                for low_y in range(2):
                    slot = jnp.where(good_ref[STATIONS_HERE] == low_y, 0, 2 * half)
                    target = pl.ds(slot + parity * half + row, PEERS, stride=4 * half)
                    out_ref[target, :] = tile[low_y * PEERS : (low_y + 1) * PEERS]


def channelise(first, count, good, samples, taps, table, earlier):
    quarter = (1, 2, 12 * LANES, 2 * OWNERS)
    out_rows = PEERS * 4 * (count // 16)
    return pl.pallas_call(
        functools.partial(channelise_kernel, first, count),
        grid=(STEPS,),
        in_specs=[
            pl.BlockSpec(memory_space=pltpu.SMEM),
            pl.BlockSpec((2, FRAMES, 2, 16, LANES), lambda q: (0, 0, 0, q, 0)),
            pl.BlockSpec((TAPS, 4 * LANES), lambda q: (0, q)),
            pl.BlockSpec((TAPS, 4 * LANES), lambda q: (0, q + STEPS)),
            pl.BlockSpec(quarter, lambda q: (q, 0, 0, 0)),
            pl.BlockSpec(memory_space=pl.ANY),
        ],
        out_specs=pl.BlockSpec((out_rows, LANES), lambda q: (0, 0)),
        out_shape=jax.ShapeDtypeStruct((out_rows, LANES), jnp.float32),
        scratch_shapes=[
            pltpu.VMEM((2, count + TAPS - 1, 16, LANES), jnp.float32),
            pltpu.VMEM((2 * 2 * 16 * count, LANES), jnp.float32),
            pltpu.VMEM((2, 2 * STATIONS_HERE * count, 12 * LANES), jnp.bfloat16),
            pltpu.VMEM((2, 2 * STATIONS_HERE * count, 2 * OWNERS), jnp.float32),
        ],
        compiler_params=pltpu.CompilerParams(vmem_limit_bytes=VMEM),
        cost_estimate=pl.CostEstimate(
            flops=125_000_000 * count, bytes_accessed=7_000_000 + 60_000 * count, transcendentals=0
        ),
        name="channelise",
    )(good, samples, taps, taps, table, earlier)


def correlate_kernel(place, *refs):
    pieces, (out_ref, stations, left, right) = (refs[:4], refs[4:8]), refs[8:]
    parity = pl.program_id(0)
    side, low_y = place[0], place[1]
    lane = lax.broadcasted_iota(jnp.int32, (PEERS // 2, LANES), 1)
    column = lax.broadcasted_iota(jnp.int32, (256, LANES), 1)

    for which in range(4):
        slot = 2 * (side if which % 2 == 0 else 1 - side)
        base = 8 * (low_y if which < 2 else 1 - low_y)
        for part, (_, count) in enumerate(PARTS):
            half = count // 16
            buffer = stations.at[slot + part]
            for core in range(2):
                for station in range(STATIONS_HERE):
                    row = parity * half + station * half // STATIONS_HERE
                    word = pieces[part][which][pl.ds(core * 2 * half + row, PEERS // 2, stride=4 * half), :]
                    if part == 1:
                        word = word if station % 2 == 0 else pltpu.roll(word, 64, 1)
                        word = jnp.where(lane < 64, word, 0.0)
                    buffer[pl.ds(base + core * 4 + station, PEERS // 2, stride=16), :] = word

    mine = pl.ds(pl.multiple_of(side * 256, 256), 256)
    for which in range(2):
        for part in range(2):
            at = [slice((2 * term + part) * LANES, (2 * term + part + 1) * LANES) for term in range(3)]
            whole = stations[2 * which + part]
            high, low = halves(whole)
            block = slice(512 * which, 512 * which + 512)
            right[block, at[0]] = high
            right[block, at[1]] = high
            right[block, at[2]] = low
            value = stations[2 * which + part, mine, :]
            if part == 0:
                swapped = pltpu.roll(value, 64, 1)
                turned = jnp.where(column < 64, swapped, -swapped)
            else:
                turned = jnp.where(
                    column < 32, pltpu.roll(value, 96, 1), jnp.where(column < 64, -pltpu.roll(value, 32, 1), 0.0)
                )
            for start, operand in ((256 * which, value), (512 + 256 * which, turned)):
                high, low = halves(operand)
                block = slice(start, start + 256)
                left[block, at[0]] = high
                left[block, at[1]] = low
                left[block, at[2]] = high

    def product(a, b):
        return lax.dot_general(a, b, (((1,), (1,)), ((), ())), preferred_element_type=jnp.float32) * (1.0 / SPECTRA)

    for at in range(0, 512, 256):
        both = [product(left[...], right[512 * q + at : 512 * q + at + 256, :]) for q in range(2)]
        real = [[both[q][256 * p : 256 * p + 256] for q in range(2)] for p in range(2)]
        imag = [[both[q][512 + 256 * p : 768 + 256 * p] for q in range(2)] for p in range(2)]
        planes = (
            real[0][0] + real[1][1],
            real[0][0] - real[1][1],
            real[0][1] + real[1][0],
            imag[0][1] - imag[1][0],
            imag[0][0] + imag[1][1],
            imag[0][0] - imag[1][1],
            imag[0][1] + imag[1][0],
            real[1][0] - real[0][1],
        )
        for index, plane in enumerate(planes):
            out_ref[0, index, :, at : at + 256] = plane.astype(jnp.bfloat16)


def correlate(place, pieces):
    specs = [pl.BlockSpec((PEERS * count // 8, LANES), lambda c: (0, 0)) for _, count in PARTS for _ in range(4)]
    return pl.pallas_call(
        correlate_kernel,
        grid=(2,),
        in_specs=[pl.BlockSpec(memory_space=pltpu.SMEM)] + specs,
        out_specs=pl.BlockSpec((1, 8, 256, 512), lambda c: (c, 0, 0, 0)),
        out_shape=jax.ShapeDtypeStruct((2, 8, 256, 512), jnp.bfloat16),
        scratch_shapes=[
            pltpu.VMEM((4, 512, LANES), jnp.float32),
            pltpu.VMEM((1024, 6 * LANES), jnp.bfloat16),
            pltpu.VMEM((1024, 6 * LANES), jnp.bfloat16),
        ],
        compiler_params=pltpu.CompilerParams(vmem_limit_bytes=SMALL_VMEM),
        cost_estimate=pl.CostEstimate(flops=3_300_000_000, bytes_accessed=8_000_000, transcendentals=0),
        name="correlate",
    )(place, *pieces)


def after(value, token):
    return pl.pallas_call(
        lambda value_ref, token_ref, out_ref: None,
        in_specs=[pl.BlockSpec(memory_space=pl.ANY), pl.BlockSpec(memory_space=pl.ANY)],
        out_specs=pl.BlockSpec(memory_space=pl.ANY),
        out_shape=jax.ShapeDtypeStruct(value.shape, value.dtype),
        input_output_aliases={0: 0},
        name="after",
    )(value, token)


def moves(sizes, target):
    pairs = []
    for z in range(sizes["z"]):
        for x in range(sizes["x"]):
            for y in range(4):
                for core in range(2):
                    source, goal = (
                        (((z * sizes["x"] + x) * 2 + at % 2) * 2 + core) * 2 + at // 2 for at in (y, target(y) % 4)
                    )
                    pairs.append((source, goal))
    return pairs


def on_device(sizes, voltages, filter_taps, input_good):
    table = jnp.asarray(transform_table())
    tile, low_y = lax.axis_index("yh"), lax.axis_index("yl")
    chan = lax.axis_index(("z", "x", "yl", "core"))
    samples = voltages.reshape(2, STATIONS_HERE, FRAMES, NCHAN // LANES, LANES)
    samples = samples.transpose(0, 2, 3, 1, 4).reshape(2, FRAMES, 2, LANES // 2, LANES)
    good = lax.dynamic_slice(input_good, (chan * STATIONS_HERE, tile), (STATIONS_HERE, 1)).reshape(STATIONS_HERE)
    good = jnp.concatenate((good, low_y.reshape(1).astype(jnp.int32)))
    swap = moves(sizes, lambda y: y + 2)
    pair = moves(sizes, lambda y: y ^ 1)
    cross = moves(sizes, lambda y: y - 1 if y % 2 == 0 else y + 1)
    pieces, earlier, token = [], filter_taps, None
    for first, count in PARTS:
        width = count // 8 * LANES
        earlier = channelise(first, count, good, samples, filter_taps, table, earlier)
        spectra = earlier if token is None else after(earlier, token)
        spectra = spectra.reshape(PEERS, 1, 2 * width)
        joined = lax.all_to_all(spectra, GROUP, split_axis=0, concat_axis=0, tiled=True)
        token = joined[0, :, :LANES]
        near, far = (joined[:, :, at : at + width].reshape(-1, LANES) for at in (0, width))
        pieces += [near] + [lax.ppermute(block, AXES, pairs) for block, pairs in ((near, swap), (far, pair), (far, cross))]
    place = jnp.stack((tile, low_y)).astype(jnp.int32)
    return correlate(place, pieces)


def solution(mesh):
    sizes = {"z": 8, "x": 4, "yl": 2, "core": 2, "yh": 2}
    fine = Mesh(mesh.devices.reshape(tuple(sizes[axis] for axis in AXES)), AXES)
    in_specs = (P(None, ("z", "x", "yl", "core"), "yh", None), P(), P())
    out_specs = P(("z", "x", "yl", "core"), None, "yh", None)
    return jax.shard_map(
        functools.partial(on_device, sizes), mesh=fine, in_specs=in_specs, out_specs=out_specs, check_vma=False
    )
```

time: 106 us -> 90.1 us (0.85)
  Pallas kernels: 48.5 us -> 41.4 us
  starting transfers between devices: 32.4 us -> 26.3 us
  local copies, waits for them, and re-layouts: 2.42 us -> 1.35 us
    all_to_all x2, starting transfers between devices: 27 us -> 18.7 us  [on_device(): lax.all_to_all(spectra, GROUP, split_axis=0, concat_axis=0, tiled=True)]
    pallas_call x3 -> x4, Pallas kernels: 48.5 us -> 41.4 us  [the longest x2 34.2 us: channelise(): pl.pallas_call(functools.partial(channelise_kernel, first, count), grid=(...]
    ppermute x2 -> x6, starting transfers between devices: 5.33 us -> 7.55 us  [on_device(): lax.ppermute(block, AXES, pairs)]
    ppermute x2 -> x6, waiting for transfers between devices: 7.46 us -> 5.73 us  [on_device(): lax.ppermute(block, AXES, pairs)]
  transfers between devices with their start and end apart: 4 -> 8, of which waited for: 2 -> 5; matrix products, arithmetic and copies ran while one was open for 0% -> 0% of each run, Pallas kernels for 17% -> 14%
where the time goes in v2:
time: 90.1 us; the launch traced here: 89.8 us
  Pallas kernels  41.4 us (46%)
  starting transfers between devices  26.3 us (29%)
  waiting for transfers between devices  20 us (22%)
  local copies, waits for them, and re-layouts  1.35 us (1%)
    pallas_call x2, Pallas kernels, channelise(): pl.pallas_call(functools.partial(channelise_kernel, first, count), grid=(...  34.2 us
    all_to_all x2, starting transfers between devices, on_device(): lax.all_to_all(spectra, GROUP, split_axis=0, concat_axis=0, tiled=True)  18.7 us
    all_to_all x2, waiting for transfers between devices, on_device(): lax.all_to_all(spectra, GROUP, split_axis=0, concat_axis=0, tiled=True)  14.3 us
    ppermute x6, starting transfers between devices, on_device(): lax.ppermute(block, AXES, pairs)  7.55 us
    pallas_call x1, Pallas kernels, correlate(): pl.pallas_call(correlate_kernel, grid=(2,), in_specs=[pl.BlockSpec(memory...  7.22 us
    ppermute x6, waiting for transfers between devices, on_device(): lax.ppermute(block, AXES, pairs)  5.73 us
  transfers between devices with their start and end apart: 8, of which 5 were waited for; matrix products, arithmetic and copies ran while one was open for 0% of the time, Pallas kernels for 14%

profile of v2, /device:TPU:1, one launch (start us, length us, event | category | flops | bytes accessed | tf_op | source)
XLA Modules:
  0.0 89.8 jit_solution(13179759049053679362)
XLA Ops:
  0.0 0.0 copy-start
  0.0 0.7 copy-done
  0.7 0.1 dynamic-slice_bitcast_fusion
  0.8 0.6 pad_add_fusion.1.good_ref
  1.4 21.4 %channelise.2.earlier = f32[1024,128]{1,0:T(8,128)} custom-call(s32[5]{0:T(128)} %pad_add_fusion.1.good_ref, bf16[2,111,2,64,128]{4,3,2,1,0:T(8,128)(2,1)} %bitcast.21, f32[16,4096]{1,0:T(8,128)} %upper_taps.3, f32[16,4096]{1,0:T(8,128)} %upper_taps.3, bf16[4,2,1536,256]{3,2,1,0:T(8,128)(2,1)} %constant.31.clone.table_ref, f32[16,4096]{1,0:T(8,128)} %upper_taps.3), custom_call_target="tpu_custom_call" | custom-call | flops 8000000000 | bytes 10840000 | tf_op jit(solution)/shard_map/channelise/pallas_call | solution.py:131
  22.8 13.0 %all-to-all-start = ((f32[64,1,2048]{2,1,0:T(1,128)}), f32[64,1,2048]{2,1,0:T(1,128)S(1)}, u32[]{:S(2)}, u32[]{:S(2)}) async-start(f32[64,1,2048]{2,1,0:T(1,128)} %bitcast.24), calls=%async_computation | async-start | bytes 1048576 | tf_op jit(solution)/shard_map/all_to_all | solution.py:286
  35.8 12.8 %channelise.3.value_ref = f32[512,128]{1,0:T(8,128)} custom-call(s32[5]{0:T(128)} %pad_add_fusion.1.good_ref, bf16[2,111,2,64,128]{4,3,2,1,0:T(8,128)(2,1)} %bitcast.22, f32[16,4096]{1,0:T(8,128)} %upper_taps.3, f32[16,4096]{1,0:T(8,128)} %upper_taps.3, bf16[4,2,1536,256]{3,2,1,0:T(8,128)(2,1)} %constant.31.clone.table_ref, f32[1024,128]{1,0:T(8,128)} %channelise.2.earlier), custom_call_target="tpu_custom_call" | custom-call | flops 4000000000 | bytes 8920000 | tf_op jit(solution)/shard_map/channelise/pallas_call | solution.py:131
  48.6 4.9 %all-to-all-done = f32[64,1,2048]{2,1,0:T(1,128)S(1)} async-done(((f32[64,1,2048]{2,1,0:T(1,128)}), f32[64,1,2048]{2,1,0:T(1,128)S(1)}, u32[]{:S(2)}, u32[]{:S(2)}) %all-to-all-start) | async-done | bytes 524320 | tf_op jit(solution)/shard_map/all_to_all | solution.py:286
  53.5 0.5 slice_bitcast_fusion.token_ref
  54.0 5.7 %all-to-all-start.1 = ((f32[64,1,1024]{2,1,0:T(1,128)}), f32[64,1,1024]{2,1,0:T(1,128)S(1)}, u32[]{:S(2)}, u32[]{:S(2)}) async-start(f32[64,1,1024]{2,1,0:T(1,128)} %bitcast.23), calls=%async_computation.1 | async-start | bytes 524288 | tf_op jit(solution)/shard_map/all_to_all | solution.py:286
  59.8 3.0 %collective-permute-start = (f32[512,128]{1,0:T(8,128)S(1)}, f32[512,128]{1,0:T(8,128)S(1)}, u32[]{:S(2)}, u32[]{:S(2)}) collective-permute-start(f32[512,128]{1,0:T(8,128)S(1)} %bitcast.17), channel_id=1, source_target_pairs={{0,1},{2,3},{4,5},{6,7},{1,0},{3,2},{5,4},{7,6},{8,9},{10,11},{12,... | collective-permute-start | bytes 786440 | tf_op jit(solution)/shard_map/ppermute | solution.py:289
  62.8 0.8 collective-permute-start.2
  63.6 0.0 collective-permute-start.1
  63.6 9.3 %all-to-all-done.1 = f32[64,1,1024]{2,1,0:T(1,128)S(1)} async-done(((f32[64,1,1024]{2,1,0:T(1,128)}), f32[64,1,1024]{2,1,0:T(1,128)S(1)}, u32[]{:S(2)}, u32[]{:S(2)}) %all-to-all-start.1) | async-done | bytes 262176 | tf_op jit(solution)/shard_map/all_to_all | solution.py:286
  73.0 3.0 %collective-permute-start.3 = (f32[256,128]{1,0:T(8,128)S(1)}, f32[256,128]{1,0:T(8,128)S(1)}, u32[]{:S(2)}, u32[]{:S(2)}) collective-permute-start(f32[256,128]{1,0:T(8,128)S(1)} %bitcast.19), channel_id=1, source_target_pairs={{0,1},{2,3},{4,5},{6,7},{1,0},{3,2},{5,4},{7,6},{8,9},{10,11},{12,... | collective-permute-start | bytes 393224 | tf_op jit(solution)/shard_map/ppermute | solution.py:289
  76.0 0.8 collective-permute-start.5
  76.8 0.0 collective-permute-done.refs_1_
  76.8 0.0 collective-permute-start.4
  76.8 0.1 pad_add_fusion.place
  76.8 0.0 collective-permute-done.2.refs_3_
  76.9 0.0 collective-permute-done.1.refs_2_
  76.9 2.6 %collective-permute-done.3.refs_5_ = f32[256,128]{1,0:T(8,128)S(1)} collective-permute-done((f32[256,128]{1,0:T(8,128)S(1)}, f32[256,128]{1,0:T(8,128)S(1)}, u32[]{:S(2)}, u32[]{:S(2)}) %collective-permute-start.3) | collective-permute-done | bytes 131104 | tf_op jit(solution)/shard_map/ppermute | solution.py:289
  79.4 2.7 %collective-permute-done.5.refs_7_ = f32[256,128]{1,0:T(8,128)S(1)} collective-permute-done((f32[256,128]{1,0:T(8,128)S(1)}, f32[256,128]{1,0:T(8,128)S(1)}, u32[]{:S(2)}, u32[]{:S(2)}) %collective-permute-start.5) | collective-permute-done | bytes 131104 | tf_op jit(solution)/shard_map/ppermute | solution.py:289
  82.1 0.4 collective-permute-done.4.refs_6_
  82.6 7.2 %correlate.1 = bf16[2,8,256,512]{3,2,1,0:T(8,128)(2,1)} custom-call(s32[2]{0:T(128)S(1)} %pad_add_fusion.place, f32[512,128]{1,0:T(8,128)S(1)} %bitcast.18, f32[512,128]{1,0:T(8,128)S(1)} %collective-permute-done.refs_1_, f32[512,128]{1,0:T(8,128)S(1)} %collective-permute-done.1.refs_2_, f32[512,128]{1,0:T(8,128)S(1)} %collective-permute-done.2.refs_3_, ...), custom_call_target="tpu_custom_call" | custom-call | flops 3300000000 | bytes 8000000 | tf_op jit(solution)/shard_map/correlate/pallas_call | solution.py:228
  (3 shorter events, 0.1 us)
Async XLA Ops:
  0.0 0.7 copy-start
  22.8 30.7 %all-to-all-start = ((f32[64,1,2048]{2,1,0:T(1,128)}), f32[64,1,2048]{2,1,0:T(1,128)S(1)}, u32[]{:S(2)}, u32[]{:S(2)}) async-start(f32[64,1,2048]{2,1,0:T(1,128)} %bitcast.24), calls=%async_computation | async-start | bytes 1048576 | tf_op jit(solution)/shard_map/all_to_all | solution.py:286
  54.0 18.9 %all-to-all-start.1 = ((f32[64,1,1024]{2,1,0:T(1,128)}), f32[64,1,1024]{2,1,0:T(1,128)S(1)}, u32[]{:S(2)}, u32[]{:S(2)}) async-start(f32[64,1,1024]{2,1,0:T(1,128)} %bitcast.23), calls=%async_computation.1 | async-start | bytes 524288 | tf_op jit(solution)/shard_map/all_to_all | solution.py:286
  59.8 16.9 %collective-permute-start = (f32[512,128]{1,0:T(8,128)S(1)}, f32[512,128]{1,0:T(8,128)S(1)}, u32[]{:S(2)}, u32[]{:S(2)}) collective-permute-start(f32[512,128]{1,0:T(8,128)S(1)} %bitcast.17), channel_id=1, source_target_pairs={{0,1},{2,3},{4,5},{6,7},{1,0},{3,2},{5,4},{7,6},{8,9},{10,11},{12,... | collective-permute-start | bytes 786440 | tf_op jit(solution)/shard_map/ppermute | solution.py:289
  62.8 14.0 %collective-permute-start.2 = (f32[512,128]{1,0:T(8,128)S(1)}, f32[512,128]{1,0:T(8,128)S(1)}, u32[]{:S(2)}, u32[]{:S(2)}) collective-permute-start(f32[512,128]{1,0:T(8,128)S(1)} %bitcast.25), channel_id=1, source_target_pairs={{0,5},{2,7},{4,1},{6,3},{1,4},{3,6},{5,0},{7,2},{8,13},{10,15},{12... | collective-permute-start | bytes 786440 | tf_op jit(solution)/shard_map/ppermute | solution.py:289
  63.6 13.3 %collective-permute-start.1 = (f32[512,128]{1,0:T(8,128)S(1)}, f32[512,128]{1,0:T(8,128)S(1)}, u32[]{:S(2)}, u32[]{:S(2)}) collective-permute-start(f32[512,128]{1,0:T(8,128)S(1)} %bitcast.26), channel_id=1, source_target_pairs={{0,4},{2,6},{4,0},{6,2},{1,5},{3,7},{5,1},{7,3},{8,12},{10,14},{12... | collective-permute-start | bytes 786440 | tf_op jit(solution)/shard_map/ppermute | solution.py:289
  73.0 6.4 %collective-permute-start.3 = (f32[256,128]{1,0:T(8,128)S(1)}, f32[256,128]{1,0:T(8,128)S(1)}, u32[]{:S(2)}, u32[]{:S(2)}) collective-permute-start(f32[256,128]{1,0:T(8,128)S(1)} %bitcast.19), channel_id=1, source_target_pairs={{0,1},{2,3},{4,5},{6,7},{1,0},{3,2},{5,4},{7,6},{8,9},{10,11},{12,... | collective-permute-start | bytes 393224 | tf_op jit(solution)/shard_map/ppermute | solution.py:289
  76.0 6.1 %collective-permute-start.5 = (f32[256,128]{1,0:T(8,128)S(1)}, f32[256,128]{1,0:T(8,128)S(1)}, u32[]{:S(2)}, u32[]{:S(2)}) collective-permute-start(f32[256,128]{1,0:T(8,128)S(1)} %bitcast.27), channel_id=1, source_target_pairs={{0,5},{2,7},{4,1},{6,3},{1,4},{3,6},{5,0},{7,2},{8,13},{10,15},{12... | collective-permute-start | bytes 393224 | tf_op jit(solution)/shard_map/ppermute | solution.py:289
  76.8 5.8 %collective-permute-start.4 = (f32[256,128]{1,0:T(8,128)S(1)}, f32[256,128]{1,0:T(8,128)S(1)}, u32[]{:S(2)}, u32[]{:S(2)}) collective-permute-start(f32[256,128]{1,0:T(8,128)S(1)} %bitcast.28), channel_id=1, source_target_pairs={{0,4},{2,6},{4,0},{6,2},{1,5},{3,7},{5,1},{7,3},{8,12},{10,14},{12... | collective-permute-start | bytes 393224 | tf_op jit(solution)/shard_map/ppermute | solution.py:289

commit v3 on v2

--- a/solution.py
+++ b/solution.py
@@ -19,6 +19,7 @@
 STEPS = 4
 OWNERS = 128
 PARTS = ((0, 64), (64, 32))
+SHORT = 4
 AXES = ("z", "x", "yl", "core", "yh")
 GROUP = ("z", "x", "core")
 PEERS = 64
@@ -44,7 +45,31 @@
     return high, low
 
 
-def channelise_kernel(first, count, good_ref, samples, lower_taps, upper_taps, table_ref, earlier, out_ref, wide, filtered, split, total):
+def fir(lines, weights, count):
+    taps = len(weights)
+    if taps <= SHORT:
+        out = []
+        for j in range(count):
+            value = weights[0] * lines[j]
+            for m in range(1, taps):
+                value = value + weights[m] * lines[j + m]
+            out.append(value)
+        return out
+    pairs = count // 2
+    even, odd = lines[0::2], lines[1::2]
+    both = [odd[t] + even[t + 1] for t in range(min(len(odd), len(even) - 1))]
+    a = fir(even, weights[0::2], pairs + 1)
+    b = fir(odd, weights[1::2], pairs)
+    c = fir(both, [u + v for u, v in zip(weights[0::2], weights[1::2])], pairs)
+    out = []
+    for t in range(pairs):
+        out += [a[t] + b[t], c[t] - a[t + 1] - b[t]]
+    if count % 2:
+        out.append(a[pairs] + fir(odd[pairs:], weights[1::2], 1)[0])
+    return out
+
+
+def channelise_kernel(count, good_ref, chan_ref, tile_ref, low_y_ref, samples, lower_taps, upper_taps, table_ref, earlier, out_ref, wide, filtered, split, total):
     step = pl.program_id(0)
     rows = STATIONS_HERE * count
     span = count + TAPS - 1
@@ -52,7 +77,7 @@
 
     def filter_part(part):
         for side, tap_ref in enumerate((lower_taps, upper_taps)):
-            wide[side] = samples[part, first : first + span, side].astype(jnp.float32)
+            wide[side] = samples[part, :, side].astype(jnp.float32)
             for pair in range(2):
                 weights = []
                 for tap in range(TAPS):
@@ -67,17 +92,9 @@
                         )
                     )
                 base = part * (8 * rows) + (side * 4 + pair * 2) * rows
-                sums = {}
-                for frame in range(span):
-                    sample = wide[side, frame, 8 * pair : 8 * pair + 8, :]
-                    for tap in range(TAPS):
-                        spectrum = frame - tap
-                        if 0 <= spectrum < count:
-                            term = sample * weights[tap]
-                            sums[spectrum] = term if tap == 0 else sums[spectrum] + term
-                    done = frame - TAPS + 1
-                    if done >= 0:
-                        filtered[pl.ds(base + done, 8, stride=count), :] = sums.pop(done)
+                lines = [wide[side, frame, 8 * pair : 8 * pair + 8, :] for frame in range(span)]
+                for spectrum, value in enumerate(fir(lines, weights, count)):
+                    filtered[pl.ds(base + spectrum, 8, stride=count), :] = value
 
     for part in range(2):
 
@@ -113,27 +130,33 @@
             imag = total[parity, rows:, :LANES] - total[parity, :rows, LANES:]
             words = []
             for station in range(STATIONS_HERE):
-                mask = good_ref[station].astype(jnp.float32)
+                mask = good_ref[tile_ref[0], chan_ref[0] * STATIONS_HERE + station].astype(jnp.float32)
                 at = slice(station * count, (station + 1) * count)
                 words += [real[at] * mask, imag[at] * mask]
             words = jnp.concatenate(words, axis=0)
             for row in range(half):
                 tile = words[row * LANES : (row + 1) * LANES].T
                 for low_y in range(2):
-                    slot = jnp.where(good_ref[STATIONS_HERE] == low_y, 0, 2 * half)
+                    slot = jnp.where(low_y_ref[0] == low_y, 0, 2 * half)
                     target = pl.ds(slot + parity * half + row, PEERS, stride=4 * half)
                     out_ref[target, :] = tile[low_y * PEERS : (low_y + 1) * PEERS]
 
 
-def channelise(first, count, good, samples, taps, table, earlier):
+def channelise(first, count, place, good, samples, taps, table, earlier):
     quarter = (1, 2, 12 * LANES, 2 * OWNERS)
     out_rows = PEERS * 4 * (count // 16)
     return pl.pallas_call(
-        functools.partial(channelise_kernel, first, count),
+        functools.partial(channelise_kernel, count),
         grid=(STEPS,),
         in_specs=[
             pl.BlockSpec(memory_space=pltpu.SMEM),
-            pl.BlockSpec((2, FRAMES, 2, 16, LANES), lambda q: (0, 0, 0, q, 0)),
+            pl.BlockSpec(memory_space=pltpu.SMEM),
+            pl.BlockSpec(memory_space=pltpu.SMEM),
+            pl.BlockSpec(memory_space=pltpu.SMEM),
+            pl.BlockSpec(
+                (pl.Element(2), pl.Element(count + TAPS - 1), pl.Element(2), pl.Element(16), pl.Element(LANES)),
+                lambda q: (0, first, 0, 16 * q, 0),
+            ),
             pl.BlockSpec((TAPS, 4 * LANES), lambda q: (0, q)),
             pl.BlockSpec((TAPS, 4 * LANES), lambda q: (0, q + STEPS)),
             pl.BlockSpec(quarter, lambda q: (q, 0, 0, 0)),
@@ -152,13 +175,13 @@
             flops=125_000_000 * count, bytes_accessed=7_000_000 + 60_000 * count, transcendentals=0
         ),
         name="channelise",
-    )(good, samples, taps, taps, table, earlier)
-
-
-def correlate_kernel(place, *refs):
+    )(good, *place, samples, taps, taps, table, earlier)
+
+
+def correlate_kernel(tile_ref, low_y_ref, *refs):
     pieces, (out_ref, stations, left, right) = (refs[:4], refs[4:8]), refs[8:]
     parity = pl.program_id(0)
-    side, low_y = place[0], place[1]
+    side, low_y = tile_ref[0], low_y_ref[0]
     lane = lax.broadcasted_iota(jnp.int32, (PEERS // 2, LANES), 1)
     column = lax.broadcasted_iota(jnp.int32, (256, LANES), 1)
 
@@ -196,14 +219,14 @@
                     column < 32, pltpu.roll(value, 96, 1), jnp.where(column < 64, -pltpu.roll(value, 32, 1), 0.0)
                 )
             for start, operand in ((256 * which, value), (512 + 256 * which, turned)):
-                high, low = halves(operand)
+                high, low = halves(operand * (1.0 / SPECTRA))
                 block = slice(start, start + 256)
                 left[block, at[0]] = high
                 left[block, at[1]] = low
                 left[block, at[2]] = high
 
     def product(a, b):
-        return lax.dot_general(a, b, (((1,), (1,)), ((), ())), preferred_element_type=jnp.float32) * (1.0 / SPECTRA)
+        return lax.dot_general(a, b, (((1,), (1,)), ((), ())), preferred_element_type=jnp.float32)
 
     for at in range(0, 512, 256):
         both = [product(left[...], right[512 * q + at : 512 * q + at + 256, :]) for q in range(2)]
@@ -223,12 +246,12 @@
             out_ref[0, index, :, at : at + 256] = plane.astype(jnp.bfloat16)
 
 
-def correlate(place, pieces):
+def correlate(tile, low_y, pieces):
     specs = [pl.BlockSpec((PEERS * count // 8, LANES), lambda c: (0, 0)) for _, count in PARTS for _ in range(4)]
     return pl.pallas_call(
         correlate_kernel,
         grid=(2,),
-        in_specs=[pl.BlockSpec(memory_space=pltpu.SMEM)] + specs,
+        in_specs=[pl.BlockSpec(memory_space=pltpu.SMEM)] * 2 + specs,
         out_specs=pl.BlockSpec((1, 8, 256, 512), lambda c: (c, 0, 0, 0)),
         out_shape=jax.ShapeDtypeStruct((2, 8, 256, 512), jnp.bfloat16),
         scratch_shapes=[
@@ -239,7 +262,7 @@
         compiler_params=pltpu.CompilerParams(vmem_limit_bytes=SMALL_VMEM),
         cost_estimate=pl.CostEstimate(flops=3_300_000_000, bytes_accessed=8_000_000, transcendentals=0),
         name="correlate",
-    )(place, *pieces)
+    )(tile, low_y, *pieces)
 
 
 def after(value, token):
@@ -272,23 +295,21 @@
     chan = lax.axis_index(("z", "x", "yl", "core"))
     samples = voltages.reshape(2, STATIONS_HERE, FRAMES, NCHAN // LANES, LANES)
     samples = samples.transpose(0, 2, 3, 1, 4).reshape(2, FRAMES, 2, LANES // 2, LANES)
-    good = lax.dynamic_slice(input_good, (chan * STATIONS_HERE, tile), (STATIONS_HERE, 1)).reshape(STATIONS_HERE)
-    good = jnp.concatenate((good, low_y.reshape(1).astype(jnp.int32)))
+    chan, tile, low_y = (index.reshape(1).astype(jnp.int32) for index in (chan, tile, low_y))
     swap = moves(sizes, lambda y: y + 2)
     pair = moves(sizes, lambda y: y ^ 1)
     cross = moves(sizes, lambda y: y - 1 if y % 2 == 0 else y + 1)
     pieces, earlier, token = [], filter_taps, None
     for first, count in PARTS:
-        width = count // 8 * LANES
-        earlier = channelise(first, count, good, samples, filter_taps, table, earlier)
+        width = count // 8
+        earlier = channelise(first, count, (chan, tile, low_y), input_good.T, samples, filter_taps, table, earlier)
         spectra = earlier if token is None else after(earlier, token)
-        spectra = spectra.reshape(PEERS, 1, 2 * width)
+        spectra = spectra.reshape(PEERS, 2 * width, LANES)
         joined = lax.all_to_all(spectra, GROUP, split_axis=0, concat_axis=0, tiled=True)
-        token = joined[0, :, :LANES]
-        near, far = (joined[:, :, at : at + width].reshape(-1, LANES) for at in (0, width))
+        token = joined[0, :8]
+        near, far = (joined[:, at : at + width].reshape(-1, LANES) for at in (0, width))
         pieces += [near] + [lax.ppermute(block, AXES, pairs) for block, pairs in ((near, swap), (far, pair), (far, cross))]
-    place = jnp.stack((tile, low_y)).astype(jnp.int32)
-    return correlate(place, pieces)
+    return correlate(tile, low_y, pieces)
 
 
 def solution(mesh):

time: 90.1 us -> 87.2 us (0.968)
  Pallas kernels: 41.4 us -> 39.4 us
    pallas_call x2, Pallas kernels: 34.2 us -> 33 us  [channelise(): pl.pallas_call(functools.partial(channelise_kernel, count), grid=(STEPS,)...]
where the time goes in v3:
time: 87.2 us; the launch traced here: 86.9 us
  Pallas kernels  39.4 us (45%)
  starting transfers between devices  26.6 us (31%)
  waiting for transfers between devices  20.2 us (23%)
    pallas_call x2, Pallas kernels, channelise(): pl.pallas_call(functools.partial(channelise_kernel, count), grid=(STEPS,)...  33 us
    all_to_all x2, starting transfers between devices, on_device(): lax.all_to_all(spectra, GROUP, split_axis=0, concat_axis=0, tiled=True)  18.7 us
    all_to_all x2, waiting for transfers between devices, on_device(): lax.all_to_all(spectra, GROUP, split_axis=0, concat_axis=0, tiled=True)  14.4 us
    ppermute x6, starting transfers between devices, on_device(): lax.ppermute(block, AXES, pairs)  7.89 us
    pallas_call x1, Pallas kernels, correlate(): pl.pallas_call(correlate_kernel, grid=(2,), in_specs=[pl.BlockSpec(memory...  6.46 us
    ppermute x6, waiting for transfers between devices, on_device(): lax.ppermute(block, AXES, pairs)  5.79 us
  transfers between devices with their start and end apart: 8, of which 5 were waited for; matrix products, arithmetic and copies ran while one was open for 0% of the time, Pallas kernels for 14%

profile of v3, /device:TPU:1, one launch (start us, length us, event | category | flops | bytes accessed | tf_op | source)
XLA Modules:
  0.0 86.9 jit_solution(4854918358263353973)
XLA Ops:
  0.0 20.6 %channelise.2.earlier = f32[1024,128]{1,0:T(8,128)} custom-call(s32[2,512]{1,0:T(2,128)} %bitcast.27, s32[1]{0:T(128)} %bitcast.3.chan_ref, s32[1]{0:T(128)} %bitcast.tile_ref, s32[1]{0:T(128)} %bitcast.1.low_y_ref, bf16[2,111,2,64,128]{4,3,2,1,0:T(8,128)(2,1)} %bitcast.21, f32[16,4096]{1,0:T(8,128)} %upper_taps.3, f32[16,4096]{1,0:T(8,128)} %upper_taps.3, ...), custom_call_target="tpu_custom_call" | custom-call | flops 8000000000 | bytes 10840000 | tf_op jit(solution)/shard_map/channelise/pallas_call | solution.py:148
  20.6 13.0 %all-to-all-start = ((f32[64,16,128]{2,1,0:T(8,128)}), f32[64,16,128]{2,1,0:T(8,128)S(1)}, u32[]{:S(2)}, u32[]{:S(2)}) async-start(f32[64,16,128]{2,1,0:T(8,128)} %bitcast.24), calls=%async_computation | async-start | bytes 1048576 | tf_op jit(solution)/shard_map/all_to_all | solution.py:308
  33.6 12.3 %channelise.3.value_ref = f32[512,128]{1,0:T(8,128)} custom-call(s32[2,512]{1,0:T(2,128)} %bitcast.28, s32[1]{0:T(128)} %bitcast.3.chan_ref, s32[1]{0:T(128)} %bitcast.tile_ref, s32[1]{0:T(128)} %bitcast.1.low_y_ref, bf16[2,111,2,64,128]{4,3,2,1,0:T(8,128)(2,1)} %bitcast.22, f32[16,4096]{1,0:T(8,128)} %upper_taps.3, f32[16,4096]{1,0:T(8,128)} %upper_taps.3, ...), custom_call_target="tpu_custom_call" | custom-call | flops 4000000000 | bytes 8920000 | tf_op jit(solution)/shard_map/channelise/pallas_call | solution.py:148
  46.0 5.4 %all-to-all-done = f32[64,16,128]{2,1,0:T(8,128)S(1)} async-done(((f32[64,16,128]{2,1,0:T(8,128)}), f32[64,16,128]{2,1,0:T(8,128)S(1)}, u32[]{:S(2)}, u32[]{:S(2)}) %all-to-all-start) | async-done | bytes 524320 | tf_op jit(solution)/shard_map/all_to_all | solution.py:308
  51.4 0.6 slice_bitcast_fusion.2.token_ref
  51.9 5.7 %all-to-all-start.1 = ((f32[64,8,128]{2,1,0:T(8,128)}), f32[64,8,128]{2,1,0:T(8,128)S(1)}, u32[]{:S(2)}, u32[]{:S(2)}) async-start(f32[64,8,128]{2,1,0:T(8,128)} %bitcast.23), calls=%async_computation.1 | async-start | bytes 524288 | tf_op jit(solution)/shard_map/all_to_all | solution.py:308
  57.7 2.8 %collective-permute-start.2 = (f32[512,128]{1,0:T(8,128)S(1)}, f32[512,128]{1,0:T(8,128)S(1)}, u32[]{:S(2)}, u32[]{:S(2)}) collective-permute-start(f32[512,128]{1,0:T(8,128)S(1)} %get-tuple-element.5), channel_id=1, source_target_pairs={{0,5},{2,7},{4,1},{6,3},{1,4},{3,6},{5,0},{7,2},{8,13},{10,15},{12... | collective-permute-start | bytes 786440 | tf_op jit(solution)/shard_map/ppermute | solution.py:311
  60.5 0.0 collective-permute-start.1
  60.5 1.3 %collective-permute-start = (f32[512,128]{1,0:T(8,128)S(1)}, f32[512,128]{1,0:T(8,128)S(1)}, u32[]{:S(2)}, u32[]{:S(2)}) collective-permute-start(f32[512,128]{1,0:T(8,128)S(1)} %get-tuple-element.6.refs_0_), channel_id=1, source_target_pairs={{0,1},{2,3},{4,5},{6,7},{1,0},{3,2},{5,4},{7,6},{8,9},{10,11},{12,... | collective-permute-start | bytes 786440 | tf_op jit(solution)/shard_map/ppermute | solution.py:311
  61.8 9.0 %all-to-all-done.1 = f32[64,8,128]{2,1,0:T(8,128)S(1)} async-done(((f32[64,8,128]{2,1,0:T(8,128)}), f32[64,8,128]{2,1,0:T(8,128)S(1)}, u32[]{:S(2)}, u32[]{:S(2)}) %all-to-all-start.1) | async-done | bytes 262176 | tf_op jit(solution)/shard_map/all_to_all | solution.py:308
  70.9 3.0 %collective-permute-start.3 = (f32[256,128]{1,0:T(8,128)S(1)}, f32[256,128]{1,0:T(8,128)S(1)}, u32[]{:S(2)}, u32[]{:S(2)}) collective-permute-start(f32[256,128]{1,0:T(8,128)S(1)} %bitcast.19), channel_id=1, source_target_pairs={{0,1},{2,3},{4,5},{6,7},{1,0},{3,2},{5,4},{7,6},{8,9},{10,11},{12,... | collective-permute-start | bytes 393224 | tf_op jit(solution)/shard_map/ppermute | solution.py:311
  73.9 0.8 collective-permute-start.5
  74.7 0.0 collective-permute-done.2.refs_3_
  74.7 0.0 collective-permute-start.4
  74.7 0.0 collective-permute-done.1.refs_2_
  74.7 0.0 collective-permute-done.refs_1_
  74.7 2.6 %collective-permute-done.3.refs_5_ = f32[256,128]{1,0:T(8,128)S(1)} collective-permute-done((f32[256,128]{1,0:T(8,128)S(1)}, f32[256,128]{1,0:T(8,128)S(1)}, u32[]{:S(2)}, u32[]{:S(2)}) %collective-permute-start.3) | collective-permute-done | bytes 131104 | tf_op jit(solution)/shard_map/ppermute | solution.py:311
  77.3 2.7 %collective-permute-done.5.refs_7_ = f32[256,128]{1,0:T(8,128)S(1)} collective-permute-done((f32[256,128]{1,0:T(8,128)S(1)}, f32[256,128]{1,0:T(8,128)S(1)}, u32[]{:S(2)}, u32[]{:S(2)}) %collective-permute-start.5) | collective-permute-done | bytes 131104 | tf_op jit(solution)/shard_map/ppermute | solution.py:311
  80.0 0.4 collective-permute-done.4.refs_6_
  80.5 6.5 %correlate.1 = bf16[2,8,256,512]{3,2,1,0:T(8,128)(2,1)} custom-call(s32[1]{0:T(128)} %bitcast.tile_ref, s32[1]{0:T(128)} %bitcast.1.low_y_ref, f32[512,128]{1,0:T(8,128)S(1)} %get-tuple-element.6.refs_0_, f32[512,128]{1,0:T(8,128)S(1)} %collective-permute-done.refs_1_, f32[512,128]{1,0:T(8,128)S(1)} %collective-permute-done.1.refs_2_, ...), custom_call_target="tpu_custom_call" | custom-call | flops 3300000000 | bytes 8000000 | tf_op jit(solution)/shard_map/correlate/pallas_call | solution.py:251
  (3 shorter events, 0.1 us)
Async XLA Ops:
  20.6 30.7 %all-to-all-start = ((f32[64,16,128]{2,1,0:T(8,128)}), f32[64,16,128]{2,1,0:T(8,128)S(1)}, u32[]{:S(2)}, u32[]{:S(2)}) async-start(f32[64,16,128]{2,1,0:T(8,128)} %bitcast.24), calls=%async_computation | async-start | bytes 1048576 | tf_op jit(solution)/shard_map/all_to_all | solution.py:308
  51.9 18.9 %all-to-all-start.1 = ((f32[64,8,128]{2,1,0:T(8,128)}), f32[64,8,128]{2,1,0:T(8,128)S(1)}, u32[]{:S(2)}, u32[]{:S(2)}) async-start(f32[64,8,128]{2,1,0:T(8,128)} %bitcast.23), calls=%async_computation.1 | async-start | bytes 524288 | tf_op jit(solution)/shard_map/all_to_all | solution.py:308
  57.7 16.9 %collective-permute-start.2 = (f32[512,128]{1,0:T(8,128)S(1)}, f32[512,128]{1,0:T(8,128)S(1)}, u32[]{:S(2)}, u32[]{:S(2)}) collective-permute-start(f32[512,128]{1,0:T(8,128)S(1)} %get-tuple-element.5), channel_id=1, source_target_pairs={{0,5},{2,7},{4,1},{6,3},{1,4},{3,6},{5,0},{7,2},{8,13},{10,15},{12... | collective-permute-start | bytes 786440 | tf_op jit(solution)/shard_map/ppermute | solution.py:311
  60.5 14.1 %collective-permute-start.1 = (f32[512,128]{1,0:T(8,128)S(1)}, f32[512,128]{1,0:T(8,128)S(1)}, u32[]{:S(2)}, u32[]{:S(2)}) collective-permute-start(f32[512,128]{1,0:T(8,128)S(1)} %get-tuple-element.5), channel_id=1, source_target_pairs={{0,4},{2,6},{4,0},{6,2},{1,5},{3,7},{5,1},{7,3},{8,12},{10,14},{12... | collective-permute-start | bytes 786440 | tf_op jit(solution)/shard_map/ppermute | solution.py:311
  60.5 14.1 %collective-permute-start = (f32[512,128]{1,0:T(8,128)S(1)}, f32[512,128]{1,0:T(8,128)S(1)}, u32[]{:S(2)}, u32[]{:S(2)}) collective-permute-start(f32[512,128]{1,0:T(8,128)S(1)} %get-tuple-element.6.refs_0_), channel_id=1, source_target_pairs={{0,1},{2,3},{4,5},{6,7},{1,0},{3,2},{5,4},{7,6},{8,9},{10,11},{12,... | collective-permute-start | bytes 786440 | tf_op jit(solution)/shard_map/ppermute | solution.py:311
  70.9 6.4 %collective-permute-start.3 = (f32[256,128]{1,0:T(8,128)S(1)}, f32[256,128]{1,0:T(8,128)S(1)}, u32[]{:S(2)}, u32[]{:S(2)}) collective-permute-start(f32[256,128]{1,0:T(8,128)S(1)} %bitcast.19), channel_id=1, source_target_pairs={{0,1},{2,3},{4,5},{6,7},{1,0},{3,2},{5,4},{7,6},{8,9},{10,11},{12,... | collective-permute-start | bytes 393224 | tf_op jit(solution)/shard_map/ppermute | solution.py:311
  73.9 6.1 %collective-permute-start.5 = (f32[256,128]{1,0:T(8,128)S(1)}, f32[256,128]{1,0:T(8,128)S(1)}, u32[]{:S(2)}, u32[]{:S(2)}) collective-permute-start(f32[256,128]{1,0:T(8,128)S(1)} %bitcast.25), channel_id=1, source_target_pairs={{0,5},{2,7},{4,1},{6,3},{1,4},{3,6},{5,0},{7,2},{8,13},{10,15},{12... | collective-permute-start | bytes 393224 | tf_op jit(solution)/shard_map/ppermute | solution.py:311
  74.7 5.8 %collective-permute-start.4 = (f32[256,128]{1,0:T(8,128)S(1)}, f32[256,128]{1,0:T(8,128)S(1)}, u32[]{:S(2)}, u32[]{:S(2)}) collective-permute-start(f32[256,128]{1,0:T(8,128)S(1)} %bitcast.26), channel_id=1, source_target_pairs={{0,4},{2,6},{4,0},{6,2},{1,5},{3,7},{5,1},{7,3},{8,12},{10,14},{12... | collective-permute-start | bytes 393224 | tf_op jit(solution)/shard_map/ppermute | solution.py:311

commit v4 on v3

--- a/solution.py
+++ b/solution.py
@@ -16,10 +16,13 @@
 FRAMES = SPECTRA + TAPS - 1
 NCHAN = 4096
 LANES = 128
-STEPS = 4
+STEPS = 2
+RADIX = 4
 OWNERS = 128
 PARTS = ((0, 64), (64, 32))
-SHORT = 4
+SHORT = 8
+BLOCK = 16
+CUT = 64
 AXES = ("z", "x", "yl", "core", "yh")
 GROUP = ("z", "x", "core")
 PEERS = 64
@@ -29,14 +32,17 @@
 
 @functools.lru_cache(maxsize=None)
 def transform_table():
-    sample = np.arange(NCHAN // 2).reshape(STEPS, 1, -1, 1)
-    owner = np.arange(OWNERS).reshape(OWNERS // 4, 2, 2).transpose(1, 0, 2)
-    channel = 2 * owner.reshape(1, 1, 1, -1) + np.arange(2).reshape(1, 2, 1, 1)
-    angle = 2.0 * np.pi / NCHAN * (sample * channel % NCHAN)
-    table = np.concatenate((np.cos(angle), np.sin(angle)), axis=-1) / math.sqrt(NCHAN)
+    sample = np.arange(NCHAN // RADIX).reshape(STEPS, 1, -1, 1)
+    order = np.arange(OWNERS // 2).reshape(OWNERS // 4, 2).T.reshape(1, 1, 1, -1)
+    rest = np.arange(RADIX).reshape(1, RADIX, 1, 1)
+    angle = 2.0 * np.pi / NCHAN * (sample * (RADIX * order + rest) % NCHAN)
+    cosine, sine = np.cos(angle) / math.sqrt(NCHAN), np.sin(angle) / math.sqrt(NCHAN)
+    real = np.concatenate((cosine, sine), axis=2)
+    imag = np.concatenate((-sine, cosine), axis=2)
+    table = np.where(rest < 2, np.concatenate((real, imag), axis=3), np.concatenate((imag, real), axis=3))
     high = table.astype(np.float32).astype(jnp.bfloat16)
     low = (table - high.astype(np.float64)).astype(np.float32).astype(jnp.bfloat16)
-    return np.concatenate((high, high, low), axis=2)
+    return np.concatenate((high, low), axis=3)
 
 
 def halves(value):
@@ -69,65 +75,94 @@
     return out
 
 
-def channelise_kernel(count, good_ref, chan_ref, tile_ref, low_y_ref, samples, lower_taps, upper_taps, table_ref, earlier, out_ref, wide, filtered, split, total):
+def channelise_kernel(count, good_ref, chan_ref, tile_ref, low_y_ref, samples, *refs):
+    taps_ref, table_ref, _, out_ref, wide, filtered, split, total, table, arrived = refs
     step = pl.program_id(0)
     rows = STATIONS_HERE * count
     span = count + TAPS - 1
     half = count // 16
 
-    def filter_part(part):
-        for side, tap_ref in enumerate((lower_taps, upper_taps)):
-            wide[side] = samples[part, :, side].astype(jnp.float32)
-            for pair in range(2):
-                weights = []
-                for tap in range(TAPS):
-                    at = 2 * pair * LANES
-                    weights.append(
-                        jnp.concatenate(
-                            (
-                                jnp.broadcast_to(tap_ref[tap : tap + 1, at : at + LANES], (4, LANES)),
-                                jnp.broadcast_to(tap_ref[tap : tap + 1, at + LANES : at + 2 * LANES], (4, LANES)),
-                            ),
-                            axis=0,
-                        )
-                    )
-                base = part * (8 * rows) + (side * 4 + pair * 2) * rows
-                lines = [wide[side, frame, 8 * pair : 8 * pair + 8, :] for frame in range(span)]
-                for spectrum, value in enumerate(fir(lines, weights, count)):
-                    filtered[pl.ds(base + spectrum, 8, stride=count), :] = value
-
-    for part in range(2):
-
-        @pl.when(step >= 0)
-        def _(part=part):
-            filter_part(part)
-
-    for part in range(2):
-        for line in range(4):
-            start = (part * 8 + line) * rows
-            one = filtered[start : start + rows, :]
-            two = filtered[start + 4 * rows : start + 5 * rows, :]
-            for parity, value in enumerate((one + two, one - two)):
-                h, l = halves(value)
-                for term, piece in enumerate((h, l, h)):
-                    at = (4 * term + line) * LANES
-                    split[parity, part * rows : (part + 1) * rows, at : at + LANES] = piece
-    for parity in range(2):
-        product = jnp.dot(split[parity], table_ref[0, parity], preferred_element_type=jnp.float32)
-
-        @pl.when(step == 0)
-        def _(parity=parity, product=product):
-            total[parity] = product
-
-        @pl.when(step > 0)
-        def _(parity=parity, product=product):
-            total[parity] += product
+    def filter_lines(index, carry):
+        part, quarter = index // RADIX, index % RADIX
+        wide[...] = samples[part, :, quarter].astype(jnp.float32)
+        for pair in range(2):
+            first = pl.multiple_of(quarter * (NCHAN // RADIX) + step * (4 * LANES) + 2 * pair * LANES, LANES)
+            near, far = taps_ref[:, pl.ds(first, LANES)], taps_ref[:, pl.ds(first + LANES, LANES)]
+            weights = [
+                jnp.concatenate(
+                    (
+                        jnp.broadcast_to(near[tap : tap + 1], (4, LANES)),
+                        jnp.broadcast_to(far[tap : tap + 1], (4, LANES)),
+                    ),
+                    axis=0,
+                )
+                for tap in range(TAPS)
+            ]
+            base = (index * 4 + pair * 2) * rows
+            for start in range(0, count, BLOCK):
+                lines = [wide[start + at, 8 * pair : 8 * pair + 8, :] for at in range(BLOCK + TAPS - 1)]
+                for spectrum, value in enumerate(fir(lines, weights, BLOCK)):
+                    filtered[pl.ds(base + start + spectrum, 8, stride=count), :] = value
+        return carry
+
+    fetch = pltpu.make_async_copy(table_ref.at[step], table, arrived)
+    fetch.start()
+    lax.fori_loop(0, 2 * RADIX, filter_lines, 0)
+
+    def split_line(index, carry):
+        line, start = index // (rows // CUT), pl.multiple_of(index % (rows // CUT) * CUT, CUT)
+
+        def samples_of(part, quarter):
+            first = pl.multiple_of(((part * RADIX + quarter) * 4 + line) * rows + start, CUT)
+            return filtered[pl.ds(first, CUT), :]
+
+        even, odd, twist = [], [], []
+        for part in range(2):
+            one, two, three, four = (samples_of(part, quarter) for quarter in range(RADIX))
+            s, u = one + three, two + four
+            even.append((s + u, s - u))
+            odd.append(one - three)
+            twist.append(two - four)
+        lines = (
+            (even[0][0], even[1][0]),
+            (odd[0] + twist[1], odd[1] - twist[0]),
+            (even[0][1], even[1][1]),
+            (odd[0] - twist[1], odd[1] + twist[0]),
+        )
+        for rest in range(RADIX):
+            for part in range(2):
+                at = pl.ds(pl.multiple_of((4 * part + line) * LANES, LANES), LANES)
+                high, low = halves(lines[rest][part])
+                split[rest, pl.ds(start, CUT), at] = high
+                split[rest, pl.ds(pl.multiple_of(rows + start, CUT), CUT), at] = low
+        return carry
+
+    lax.fori_loop(0, 4 * (rows // CUT), split_line, 0)
+
+    @pl.when(step == 0)
+    def _():
+        total[...] = jnp.zeros_like(total)
+
+    fetch.wait()
+
+    def transform(rest, carry):
+        total[rest] += jnp.dot(split[rest], table[rest], preferred_element_type=jnp.float32)
+        return carry
+
+    lax.fori_loop(0, RADIX, transform, 0)
 
     @pl.when(step == STEPS - 1)
     def _():
+        lane = lax.broadcasted_iota(jnp.int32, (rows, LANES), 1)
+
+        def summed(rest):
+            both = total[rest, :rows, :] + total[rest, rows:, :]
+            return both[:, :LANES] + both[:, LANES:]
+
         for parity in range(2):
-            real = total[parity, :rows, :LANES] + total[parity, rows:, LANES:]
-            imag = total[parity, rows:, :LANES] - total[parity, :rows, LANES:]
+            one, two = summed(parity), summed(parity + 2)
+            real = jnp.where(lane < 64, one, two)
+            imag = pltpu.roll(jnp.where(lane < 64, two, one), 64, 1)
             words = []
             for station in range(STATIONS_HERE):
                 mask = good_ref[tile_ref[0], chan_ref[0] * STATIONS_HERE + station].astype(jnp.float32)
@@ -136,14 +171,15 @@
             words = jnp.concatenate(words, axis=0)
             for row in range(half):
                 tile = words[row * LANES : (row + 1) * LANES].T
-                for low_y in range(2):
-                    slot = jnp.where(low_y_ref[0] == low_y, 0, 2 * half)
-                    target = pl.ds(slot + parity * half + row, PEERS, stride=4 * half)
-                    out_ref[target, :] = tile[low_y * PEERS : (low_y + 1) * PEERS]
+                for core in range(2):
+                    for low_y in range(2):
+                        slot = jnp.where(low_y_ref[0] == low_y, 0, 2 * half) + core * 4 * half
+                        target = pl.ds(slot + parity * half + row, PEERS // 2, stride=8 * half)
+                        start = (2 * core + low_y) * (PEERS // 2)
+                        out_ref[target, :] = tile[start : start + PEERS // 2]
 
 
 def channelise(first, count, place, good, samples, taps, table, earlier):
-    quarter = (1, 2, 12 * LANES, 2 * OWNERS)
     out_rows = PEERS * 4 * (count // 16)
     return pl.pallas_call(
         functools.partial(channelise_kernel, count),
@@ -154,28 +190,29 @@
             pl.BlockSpec(memory_space=pltpu.SMEM),
             pl.BlockSpec(memory_space=pltpu.SMEM),
             pl.BlockSpec(
-                (pl.Element(2), pl.Element(count + TAPS - 1), pl.Element(2), pl.Element(16), pl.Element(LANES)),
+                (pl.Element(2), pl.Element(count + TAPS - 1), pl.Element(RADIX), pl.Element(16), pl.Element(LANES)),
                 lambda q: (0, first, 0, 16 * q, 0),
             ),
-            pl.BlockSpec((TAPS, 4 * LANES), lambda q: (0, q)),
-            pl.BlockSpec((TAPS, 4 * LANES), lambda q: (0, q + STEPS)),
-            pl.BlockSpec(quarter, lambda q: (q, 0, 0, 0)),
+            pl.BlockSpec((TAPS, NCHAN), lambda q: (0, 0)),
+            pl.BlockSpec(memory_space=pl.ANY),
             pl.BlockSpec(memory_space=pl.ANY),
         ],
         out_specs=pl.BlockSpec((out_rows, LANES), lambda q: (0, 0)),
         out_shape=jax.ShapeDtypeStruct((out_rows, LANES), jnp.float32),
         scratch_shapes=[
-            pltpu.VMEM((2, count + TAPS - 1, 16, LANES), jnp.float32),
-            pltpu.VMEM((2 * 2 * 16 * count, LANES), jnp.float32),
-            pltpu.VMEM((2, 2 * STATIONS_HERE * count, 12 * LANES), jnp.bfloat16),
-            pltpu.VMEM((2, 2 * STATIONS_HERE * count, 2 * OWNERS), jnp.float32),
+            pltpu.VMEM((count + TAPS - 1, 16, LANES), jnp.float32),
+            pltpu.VMEM((2 * RADIX * 16 * count, LANES), jnp.float32),
+            pltpu.VMEM((RADIX, 2 * STATIONS_HERE * count, 8 * LANES), jnp.bfloat16),
+            pltpu.VMEM((RADIX, 2 * STATIONS_HERE * count, 2 * LANES), jnp.float32),
+            pltpu.VMEM((RADIX, 8 * LANES, 2 * LANES), jnp.bfloat16),
+            pltpu.SemaphoreType.DMA,
         ],
         compiler_params=pltpu.CompilerParams(vmem_limit_bytes=VMEM),
         cost_estimate=pl.CostEstimate(
             flops=125_000_000 * count, bytes_accessed=7_000_000 + 60_000 * count, transcendentals=0
         ),
         name="channelise",
-    )(good, *place, samples, taps, taps, table, earlier)
+    )(good, *place, samples, taps, table, earlier)
 
 
 def correlate_kernel(tile_ref, low_y_ref, *refs):
@@ -294,7 +331,7 @@
     tile, low_y = lax.axis_index("yh"), lax.axis_index("yl")
     chan = lax.axis_index(("z", "x", "yl", "core"))
     samples = voltages.reshape(2, STATIONS_HERE, FRAMES, NCHAN // LANES, LANES)
-    samples = samples.transpose(0, 2, 3, 1, 4).reshape(2, FRAMES, 2, LANES // 2, LANES)
+    samples = samples.transpose(0, 2, 3, 1, 4).reshape(2, FRAMES, RADIX, LANES // RADIX, LANES)
     chan, tile, low_y = (index.reshape(1).astype(jnp.int32) for index in (chan, tile, low_y))
     swap = moves(sizes, lambda y: y + 2)
     pair = moves(sizes, lambda y: y ^ 1)

time: 87.2 us -> 85.3 us (0.978)
  Pallas kernels: 39.4 us -> 36.5 us
  waiting for transfers between devices: 20.2 us -> 21.3 us
    pallas_call x2, Pallas kernels: 33 us -> 30 us  [channelise(): pl.pallas_call(functools.partial(channelise_kernel, count), grid=(STEPS,)...]
    all_to_all x2, waiting for transfers between devices: 14.4 us -> 15.5 us  [on_device(): lax.all_to_all(spectra, GROUP, split_axis=0, concat_axis=0, tiled=True)]
  transfers between devices with their start and end apart: 8 -> 8, of which waited for: 5 -> 5; matrix products, arithmetic and copies ran while one was open for 0% -> 0% of each run, Pallas kernels for 14% -> 13%
where the time goes in v4:
time: 85.3 us; the launch traced here: 85.1 us
  Pallas kernels  36.5 us (43%)
  starting transfers between devices  26.6 us (31%)
  waiting for transfers between devices  21.3 us (25%)
    pallas_call x2, Pallas kernels, channelise(): pl.pallas_call(functools.partial(channelise_kernel, count), grid=(STEPS,)...  30 us
    all_to_all x2, starting transfers between devices, on_device(): lax.all_to_all(spectra, GROUP, split_axis=0, concat_axis=0, tiled=True)  18.7 us
    all_to_all x2, waiting for transfers between devices, on_device(): lax.all_to_all(spectra, GROUP, split_axis=0, concat_axis=0, tiled=True)  15.5 us
    ppermute x6, starting transfers between devices, on_device(): lax.ppermute(block, AXES, pairs)  7.89 us
    pallas_call x1, Pallas kernels, correlate(): pl.pallas_call(correlate_kernel, grid=(2,), in_specs=[pl.BlockSpec(memory...  6.46 us
    ppermute x6, waiting for transfers between devices, on_device(): lax.ppermute(block, AXES, pairs)  5.79 us
  transfers between devices with their start and end apart: 8, of which 5 were waited for; matrix products, arithmetic and copies ran while one was open for 0% of the time, Pallas kernels for 13%

profile of v4, /device:TPU:1, one launch (start us, length us, event | category | flops | bytes accessed | tf_op | source)
XLA Modules:
  0.0 85.1 jit_solution(4480869362651672352)
XLA Ops:
  0.0 18.8 %channelise.2.refs_2_ = f32[1024,128]{1,0:T(8,128)} custom-call(s32[2,512]{1,0:T(2,128)} %bitcast.27, s32[1]{0:T(128)} %bitcast.3.chan_ref, s32[1]{0:T(128)} %bitcast.tile_ref, s32[1]{0:T(128)} %bitcast.1.low_y_ref, bf16[2,111,4,32,128]{4,3,2,1,0:T(8,128)(2,1)} %bitcast.25, f32[16,4096]{1,0:T(8,128)} %refs_0_.3, ...), custom_call_target="tpu_custom_call" | custom-call | flops 8000000000 | bytes 10840000 | tf_op jit(solution)/shard_map/channelise/pallas_call | solution.py:184
  18.8 13.0 %all-to-all-start = ((f32[64,16,128]{2,1,0:T(8,128)}), f32[64,16,128]{2,1,0:T(8,128)S(1)}, u32[]{:S(2)}, u32[]{:S(2)}) async-start(f32[64,16,128]{2,1,0:T(8,128)} %bitcast.22), calls=%async_computation | async-start | bytes 1048576 | tf_op jit(solution)/shard_map/all_to_all | solution.py:345
  31.8 11.3 %channelise.3.value_ref = f32[512,128]{1,0:T(8,128)} custom-call(s32[2,512]{1,0:T(2,128)} %bitcast.28, s32[1]{0:T(128)} %bitcast.3.chan_ref, s32[1]{0:T(128)} %bitcast.tile_ref, s32[1]{0:T(128)} %bitcast.1.low_y_ref, bf16[2,111,4,32,128]{4,3,2,1,0:T(8,128)(2,1)} %bitcast.26, f32[16,4096]{1,0:T(8,128)} %refs_0_.3, ...), custom_call_target="tpu_custom_call" | custom-call | flops 4000000000 | bytes 8920000 | tf_op jit(solution)/shard_map/channelise/pallas_call | solution.py:184
  43.0 6.5 %all-to-all-done = f32[64,16,128]{2,1,0:T(8,128)S(1)} async-done(((f32[64,16,128]{2,1,0:T(8,128)}), f32[64,16,128]{2,1,0:T(8,128)S(1)}, u32[]{:S(2)}, u32[]{:S(2)}) %all-to-all-start) | async-done | bytes 524320 | tf_op jit(solution)/shard_map/all_to_all | solution.py:345
  49.5 0.6 slice_bitcast_fusion.2.token_ref
  50.1 5.7 %all-to-all-start.1 = ((f32[64,8,128]{2,1,0:T(8,128)}), f32[64,8,128]{2,1,0:T(8,128)S(1)}, u32[]{:S(2)}, u32[]{:S(2)}) async-start(f32[64,8,128]{2,1,0:T(8,128)} %bitcast.21), calls=%async_computation.1 | async-start | bytes 524288 | tf_op jit(solution)/shard_map/all_to_all | solution.py:345
  55.9 2.8 %collective-permute-start.2 = (f32[512,128]{1,0:T(8,128)S(1)}, f32[512,128]{1,0:T(8,128)S(1)}, u32[]{:S(2)}, u32[]{:S(2)}) collective-permute-start(f32[512,128]{1,0:T(8,128)S(1)} %get-tuple-element.5), channel_id=1, source_target_pairs={{0,5},{2,7},{4,1},{6,3},{1,4},{3,6},{5,0},{7,2},{8,13},{10,15},{12... | collective-permute-start | bytes 786440 | tf_op jit(solution)/shard_map/ppermute | solution.py:348
  58.7 0.0 collective-permute-start.1
  58.7 1.3 %collective-permute-start = (f32[512,128]{1,0:T(8,128)S(1)}, f32[512,128]{1,0:T(8,128)S(1)}, u32[]{:S(2)}, u32[]{:S(2)}) collective-permute-start(f32[512,128]{1,0:T(8,128)S(1)} %get-tuple-element.6.refs_0_), channel_id=1, source_target_pairs={{0,1},{2,3},{4,5},{6,7},{1,0},{3,2},{5,4},{7,6},{8,9},{10,11},{12,... | collective-permute-start | bytes 786440 | tf_op jit(solution)/shard_map/ppermute | solution.py:348
  60.0 9.0 %all-to-all-done.1 = f32[64,8,128]{2,1,0:T(8,128)S(1)} async-done(((f32[64,8,128]{2,1,0:T(8,128)}), f32[64,8,128]{2,1,0:T(8,128)S(1)}, u32[]{:S(2)}, u32[]{:S(2)}) %all-to-all-start.1) | async-done | bytes 262176 | tf_op jit(solution)/shard_map/all_to_all | solution.py:345
  69.0 3.0 %collective-permute-start.3 = (f32[256,128]{1,0:T(8,128)S(1)}, f32[256,128]{1,0:T(8,128)S(1)}, u32[]{:S(2)}, u32[]{:S(2)}) collective-permute-start(f32[256,128]{1,0:T(8,128)S(1)} %bitcast.19), channel_id=1, source_target_pairs={{0,1},{2,3},{4,5},{6,7},{1,0},{3,2},{5,4},{7,6},{8,9},{10,11},{12,... | collective-permute-start | bytes 393224 | tf_op jit(solution)/shard_map/ppermute | solution.py:348
  72.0 0.8 collective-permute-start.5
  72.8 0.0 collective-permute-done.2.refs_3_
  72.8 0.0 collective-permute-start.4
  72.8 0.0 collective-permute-done.1.refs_2_
  72.8 0.0 collective-permute-done.refs_1_
  72.8 2.6 %collective-permute-done.3.refs_5_ = f32[256,128]{1,0:T(8,128)S(1)} collective-permute-done((f32[256,128]{1,0:T(8,128)S(1)}, f32[256,128]{1,0:T(8,128)S(1)}, u32[]{:S(2)}, u32[]{:S(2)}) %collective-permute-start.3) | collective-permute-done | bytes 131104 | tf_op jit(solution)/shard_map/ppermute | solution.py:348
  75.5 2.7 %collective-permute-done.5.refs_7_ = f32[256,128]{1,0:T(8,128)S(1)} collective-permute-done((f32[256,128]{1,0:T(8,128)S(1)}, f32[256,128]{1,0:T(8,128)S(1)}, u32[]{:S(2)}, u32[]{:S(2)}) %collective-permute-start.5) | collective-permute-done | bytes 131104 | tf_op jit(solution)/shard_map/ppermute | solution.py:348
  78.2 0.4 collective-permute-done.4.refs_6_
  78.6 6.5 %correlate.1 = bf16[2,8,256,512]{3,2,1,0:T(8,128)(2,1)} custom-call(s32[1]{0:T(128)} %bitcast.tile_ref, s32[1]{0:T(128)} %bitcast.1.low_y_ref, f32[512,128]{1,0:T(8,128)S(1)} %get-tuple-element.6.refs_0_, f32[512,128]{1,0:T(8,128)S(1)} %collective-permute-done.refs_1_, f32[512,128]{1,0:T(8,128)S(1)} %collective-permute-done.1.refs_2_, ...), custom_call_target="tpu_custom_call" | custom-call | flops 3300000000 | bytes 8000000 | tf_op jit(solution)/shard_map/correlate/pallas_call | solution.py:288
  (3 shorter events, 0.1 us)
Async XLA Ops:
  18.8 30.7 %all-to-all-start = ((f32[64,16,128]{2,1,0:T(8,128)}), f32[64,16,128]{2,1,0:T(8,128)S(1)}, u32[]{:S(2)}, u32[]{:S(2)}) async-start(f32[64,16,128]{2,1,0:T(8,128)} %bitcast.22), calls=%async_computation | async-start | bytes 1048576 | tf_op jit(solution)/shard_map/all_to_all | solution.py:345
  50.1 18.9 %all-to-all-start.1 = ((f32[64,8,128]{2,1,0:T(8,128)}), f32[64,8,128]{2,1,0:T(8,128)S(1)}, u32[]{:S(2)}, u32[]{:S(2)}) async-start(f32[64,8,128]{2,1,0:T(8,128)} %bitcast.21), calls=%async_computation.1 | async-start | bytes 524288 | tf_op jit(solution)/shard_map/all_to_all | solution.py:345
  55.9 16.9 %collective-permute-start.2 = (f32[512,128]{1,0:T(8,128)S(1)}, f32[512,128]{1,0:T(8,128)S(1)}, u32[]{:S(2)}, u32[]{:S(2)}) collective-permute-start(f32[512,128]{1,0:T(8,128)S(1)} %get-tuple-element.5), channel_id=1, source_target_pairs={{0,5},{2,7},{4,1},{6,3},{1,4},{3,6},{5,0},{7,2},{8,13},{10,15},{12... | collective-permute-start | bytes 786440 | tf_op jit(solution)/shard_map/ppermute | solution.py:348
  58.7 14.1 %collective-permute-start.1 = (f32[512,128]{1,0:T(8,128)S(1)}, f32[512,128]{1,0:T(8,128)S(1)}, u32[]{:S(2)}, u32[]{:S(2)}) collective-permute-start(f32[512,128]{1,0:T(8,128)S(1)} %get-tuple-element.5), channel_id=1, source_target_pairs={{0,4},{2,6},{4,0},{6,2},{1,5},{3,7},{5,1},{7,3},{8,12},{10,14},{12... | collective-permute-start | bytes 786440 | tf_op jit(solution)/shard_map/ppermute | solution.py:348
  58.7 14.1 %collective-permute-start = (f32[512,128]{1,0:T(8,128)S(1)}, f32[512,128]{1,0:T(8,128)S(1)}, u32[]{:S(2)}, u32[]{:S(2)}) collective-permute-start(f32[512,128]{1,0:T(8,128)S(1)} %get-tuple-element.6.refs_0_), channel_id=1, source_target_pairs={{0,1},{2,3},{4,5},{6,7},{1,0},{3,2},{5,4},{7,6},{8,9},{10,11},{12,... | collective-permute-start | bytes 786440 | tf_op jit(solution)/shard_map/ppermute | solution.py:348
  69.0 6.4 %collective-permute-start.3 = (f32[256,128]{1,0:T(8,128)S(1)}, f32[256,128]{1,0:T(8,128)S(1)}, u32[]{:S(2)}, u32[]{:S(2)}) collective-permute-start(f32[256,128]{1,0:T(8,128)S(1)} %bitcast.19), channel_id=1, source_target_pairs={{0,1},{2,3},{4,5},{6,7},{1,0},{3,2},{5,4},{7,6},{8,9},{10,11},{12,... | collective-permute-start | bytes 393224 | tf_op jit(solution)/shard_map/ppermute | solution.py:348
  72.0 6.1 %collective-permute-start.5 = (f32[256,128]{1,0:T(8,128)S(1)}, f32[256,128]{1,0:T(8,128)S(1)}, u32[]{:S(2)}, u32[]{:S(2)}) collective-permute-start(f32[256,128]{1,0:T(8,128)S(1)} %bitcast.23), channel_id=1, source_target_pairs={{0,5},{2,7},{4,1},{6,3},{1,4},{3,6},{5,0},{7,2},{8,13},{10,15},{12... | collective-permute-start | bytes 393224 | tf_op jit(solution)/shard_map/ppermute | solution.py:348
  72.8 5.8 %collective-permute-start.4 = (f32[256,128]{1,0:T(8,128)S(1)}, f32[256,128]{1,0:T(8,128)S(1)}, u32[]{:S(2)}, u32[]{:S(2)}) collective-permute-start(f32[256,128]{1,0:T(8,128)S(1)} %bitcast.24), channel_id=1, source_target_pairs={{0,4},{2,6},{4,0},{6,2},{1,5},{3,7},{5,1},{7,3},{8,12},{10,14},{12... | collective-permute-start | bytes 393224 | tf_op jit(solution)/shard_map/ppermute | solution.py:348
